TPU v7x, 32 devices: a whole 2x2x4 slice. The times are simulated.
32 devices in a mesh: outer: 8 (over z, x), inner: 4 (over y, core).
Axes of the slice: x: 2, y: 2, z: 4, core: 2. Of those that a mesh axis runs over, the one named last changes fastest.
Arguments:
- query_in: bfloat16 [4096, 1024], P(('outer', 'inner')), may hold values from -6 to 6
- key_in: bfloat16 [4096, 1024], P(('outer', 'inner')), may hold values from -6 to 6
- value_in: bfloat16 [4096, 1024], P(('outer', 'inner')), may hold values from -6 to 6
- conv_taps: float32 [3, 3, 1024], replicated, may hold values from -3.5 to 3.5
- long_filter: float32 [4096, 1024], P(('outer', 'inner')), may hold values from -1.1 to 1.1
- skip_gain: float32 [1024], replicated, may hold values from 0.5 to 1.5
- grad_out: bfloat16 [4096, 1024], P(('outer', 'inner')), may hold values from -6 to 6
Outputs:
- output: bfloat16 [4096, 1024], P(('outer', 'inner'))
- grad_query: bfloat16 [4096, 1024], P(('outer', 'inner'))
- grad_key: bfloat16 [4096, 1024], P(('outer', 'inner'))
- grad_value: bfloat16 [4096, 1024], P(('outer', 'inner'))
All inputs are finite; a program needn't handle non-finite values.
Results may differ from a plain program's by a relative error of at most 0.001.
Values may be sent and summed in bfloat16 or wider, within the bound.
No kernel may reach another device: no remote copies, remote signals or barrier semaphores. Data moves between devices by JAX's collectives and lax.ppermute only.
A program may use at most 64 MiB of HBM per device.

v0:
```python
import functools
import math

import jax
import jax.numpy as jnp
import ml_dtypes
import numpy as np
from jax import lax
from jax.experimental import pallas as pl
from jax.experimental.pallas import tpu as pltpu
from jax.sharding import PartitionSpec as P

AXES = ("outer", "inner")
f32 = jnp.float32
bf16 = jnp.bfloat16
VMEM_LIMIT = 56 * 1024 * 1024

OUTER_SLOPE = 4.0


class Code:
    def __init__(self, low, high, slope, top):
        self.low, self.high, self.slope = low, high, slope
        self.at_high = 126.0 - OUTER_SLOPE * (top - high)
        self.at_low = self.at_high - slope * (high - low)

    def encode(self, value):
        place = jnp.log2(jnp.abs(value))
        inside = jnp.clip(place, self.low, self.high)
        code = OUTER_SLOPE * place + ((self.slope - OUTER_SLOPE) * inside + self.shift())
        size = jnp.exp2(code)
        return jnp.where(value < 0, -size, size)

    def decode(self, word):
        code = jnp.log2(jnp.abs(word))
        inside = jnp.clip(code, self.at_low, self.at_high)
        place = (1.0 / OUTER_SLOPE) * code + (
            (1.0 / self.slope - 1.0 / OUTER_SLOPE) * inside + self.back_shift()
        )
        size = jnp.exp2(place)
        return jnp.where(word < 0, -size, size)

    def shift(self):
        return self.at_high - self.slope * self.high

    def back_shift(self):
        return self.high - self.at_high / self.slope


def split_pair(value):
    high = value.astype(bf16)
    return high, (value - high.astype(f32)).astype(bf16)


def numpy_pair(value):
    high = value.astype(np.float32).astype(ml_dtypes.bfloat16)
    low = (value - high.astype(np.float64)).astype(np.float32).astype(ml_dtypes.bfloat16)
    return high, low


def dot(left, right):
    return jnp.dot(left, right, preferred_element_type=f32)


def dot_pair(left, right):
    return dot(left[0], right[0]) + (dot(left[0], right[1]) + dot(left[1], right[0]))


@functools.lru_cache(maxsize=None)
def tables(blocks, rows, unit):
    points = 2 * blocks * rows
    bins = np.arange(blocks) + 0.5
    angle = np.outer(bins, np.arange(blocks)) * (2 * math.pi / (2 * blocks))
    eye = np.eye(unit)
    coarse = np.concatenate([np.kron(np.cos(angle), eye), np.kron(-np.sin(angle), eye)], axis=0)
    coarse_back = np.concatenate(
        [np.kron(np.cos(angle).T, eye), np.kron(-np.sin(angle).T, eye)], axis=1
    ) * (2.0 / points)
    twist = np.repeat(np.outer(bins, np.arange(rows)) * (2 * math.pi / points), unit, axis=0)
    fine = np.outer(np.arange(rows), np.arange(rows)) * (2 * math.pi / rows)
    cos, sin = np.cos(fine), np.sin(fine)
    forward = np.block([[cos, -sin], [sin, cos]])
    backward = np.block([[cos, sin], [-sin, cos]])
    pairs = [numpy_pair(table) for table in (coarse, coarse_back, forward, backward)]
    flat = [half for pair in pairs for half in pair]
    return flat + [np.cos(twist).astype(np.float32), np.sin(twist).astype(np.float32)]


def shifted(stream, steps, rim):
    rolled = pltpu.roll(stream, steps, 0)
    row = lax.broadcasted_iota(jnp.int32, stream.shape, 0)
    if steps == 1:
        return jnp.where(row == 0, rim[1:2], rolled)
    return jnp.where(row == 0, rim[0:1], jnp.where(row == 1, rim[1:2], rolled))


def short_forward(stream, taps, which, rim):
    return (
        taps[3 * which : 3 * which + 1] * stream
        + taps[3 * which + 1 : 3 * which + 2] * shifted(stream, 1, rim)
        + taps[3 * which + 2 : 3 * which + 3] * shifted(stream, 2, rim)
    )


def ahead(rows, steps):
    count = rows.shape[0]
    rolled = pltpu.roll(rows, count - steps, 0)
    row = lax.broadcasted_iota(jnp.int32, rows.shape, 0)
    return jnp.where(row < count - steps, rolled, 0.0)


def gate_kernel(code, groups, q_ref, k_ref, v_ref, g_ref, h_ref, rim_ref, taps_ref, out_ref, held):
    rows, channels = q_ref.shape
    count = channels // groups
    chunk = min(128, count)
    for start in range(0, channels, chunk):
        lanes = pl.ds(start, chunk)
        taps = taps_ref[:, lanes]
        rim = rim_ref[:, lanes].astype(f32)
        short_q = short_forward(q_ref[:, lanes].astype(f32), taps, 0, rim[0:2])
        short_k = short_forward(k_ref[:, lanes].astype(f32), taps, 1, rim[2:4])
        short_v = short_forward(v_ref[:, lanes].astype(f32), taps, 2, rim[4:6])
        signals = (
            short_k * short_v,
            h_ref[:, lanes] * 32.0,
            g_ref[:, lanes].astype(f32) * short_q,
        )
        for which, signal in enumerate(signals):
            word = code.encode(signal).T
            if groups == 1:
                held[which, pl.ds(start, chunk), :] = word
            else:
                group, first = start // count, start % count // 8
                held[which, pl.ds(first, chunk // 8), pl.ds(8 * group, 8), :] = word.reshape(
                    chunk // 8, 8, rows
                )
    for which in range(3):
        out_ref[which] = held[which].reshape(channels, rows).astype(bf16)


def transform_kernel(code_in, code_out, groups, *refs):
    x_ref = refs[0]
    table_refs = refs[1:11]
    out_ref, held, back = refs[11:]
    channels, rows = x_ref.shape[1:]
    count = channels // groups
    for which in range(3):
        words = code_in.decode(x_ref[which].astype(f32))
        held[which] = words.reshape(held.shape[1:])

    def one_group(group):
        def take(which):
            if groups == 1:
                return held[which]
            return held[which, :, pl.ds(8 * group, 8), :].reshape(count, rows)

        coarse = (table_refs[0][...], table_refs[1][...])
        coarse_back = (table_refs[2][...], table_refs[3][...])
        forward = (table_refs[4][...], table_refs[5][...])
        backward = (table_refs[6][...], table_refs[7][...])
        cos, sin = table_refs[8][...], table_refs[9][...]
        stacked = jnp.concatenate([take(0), take(1), take(2)], axis=1)
        first = dot_pair(coarse, split_pair(stacked))
        spectra = []
        for which in range(3):
            real = first[:count, which * rows : (which + 1) * rows]
            imag = first[count:, which * rows : (which + 1) * rows]
            turned = jnp.concatenate([real * cos + imag * sin, imag * cos - real * sin], axis=1)
            spectrum = dot_pair(split_pair(turned), forward)
            spectra.append((spectrum[:, :rows], spectrum[:, rows:]))
        (gr, gi), (hr, hi), (mr, mi) = spectra
        products = (
            (gr * hr - gi * hi, gr * hi + gi * hr),
            (mr * hr + mi * hi, mi * hr - mr * hi),
        )
        lasts = []
        for real, imag in products:
            product = jnp.concatenate([real, imag], axis=1)
            plain = dot_pair(split_pair(product), backward)
            real, imag = plain[:, :rows], plain[:, rows:]
            lasts.append(
                jnp.concatenate([real * cos - imag * sin, imag * cos + real * sin], axis=0)
            )
        result = dot_pair(coarse_back, split_pair(jnp.concatenate(lasts, axis=1)))
        result = result * (1.0 / 32.0)
        for which in range(2):
            part = result[:, which * rows : (which + 1) * rows]
            if groups == 1:
                back[which] = part
            else:
                back[which, :, pl.ds(8 * group, 8), :] = part.reshape(count // 8, 8, rows)

    for group in range(groups):
        one_group(group)
    for which in range(2):
        out_ref[which] = code_out.encode(back[which].reshape(channels, rows)).astype(bf16)


def finish_kernel(
    code,
    groups,
    y_ref,
    q_ref,
    k_ref,
    v_ref,
    g_ref,
    rim_ref,
    taps_ref,
    skip_ref,
    out_ref,
    gq_ref,
    gk_ref,
    gv_ref,
    first_ref,
    last_ref,
    held,
):
    rows, channels = q_ref.shape
    count = channels // groups
    chunk = min(128, count)
    for which in range(2):
        held[which] = code.decode(y_ref[which].astype(f32)).reshape(held.shape[1:])
    for start in range(0, channels, chunk):
        lanes = pl.ds(start, chunk)
        taps = taps_ref[:, lanes]
        skip = skip_ref[:, lanes]
        rim = rim_ref[:, lanes].astype(f32)

        def arrived(which):
            if groups == 1:
                return held[which, pl.ds(start, chunk), :].T
            group, first = start // count, start % count // 8
            part = held[which, pl.ds(first, chunk // 8), pl.ds(8 * group, 8), :]
            return part.reshape(chunk, rows).T

        short_q = short_forward(q_ref[:, lanes].astype(f32), taps, 0, rim[0:2])
        short_k = short_forward(k_ref[:, lanes].astype(f32), taps, 1, rim[2:4])
        short_v = short_forward(v_ref[:, lanes].astype(f32), taps, 2, rim[4:6])
        upstream = g_ref[:, lanes].astype(f32)
        mixed = arrived(0) + skip * (short_k * short_v)
        out_ref[:, lanes] = (short_q * mixed).astype(bf16)
        grad_gated = arrived(1) + skip * (upstream * short_q)
        grads = (upstream * mixed, grad_gated * short_v, grad_gated * short_k)
        for which, (rows_of, ref) in enumerate(zip(grads, (gq_ref, gk_ref, gv_ref))):
            total = (
                taps[3 * which : 3 * which + 1] * rows_of
                + taps[3 * which + 1 : 3 * which + 2] * ahead(rows_of, 1)
                + taps[3 * which + 2 : 3 * which + 3] * ahead(rows_of, 2)
            )
            ref[:, lanes] = total.astype(bf16)
            first_ref[2 * which : 2 * which + 2, lanes] = rows_of[0:2]
            last_ref[2 * which : 2 * which + 2, lanes] = total[rows - 2 :]


def rim_kernel(gq_ref, gk_ref, gv_ref, last_ref, later_ref, taps_ref, oq_ref, ok_ref, ov_ref):
    block = gq_ref.shape[0]
    row = lax.broadcasted_iota(jnp.int32, gq_ref.shape, 0)
    pairs = ((gq_ref, oq_ref), (gk_ref, ok_ref), (gv_ref, ov_ref))
    for which, (ref, out) in enumerate(pairs):
        one, two = taps_ref[3 * which + 1 : 3 * which + 2], taps_ref[3 * which + 2 : 3 * which + 3]
        at = 2 * which
        upper = last_ref[at : at + 1] + two * later_ref[at : at + 1]
        lower = (
            last_ref[at + 1 : at + 2]
            + one * later_ref[at : at + 1]
            + two * later_ref[at + 1 : at + 2]
        )
        value = ref[...].astype(f32)
        value = jnp.where(row == block - 2, upper, jnp.where(row == block - 1, lower, value))
        out[...] = value.astype(bf16)


def from_behind(value, steps):
    count = lax.axis_size(AXES)
    initial, last = max(0, -steps), min(count, count - steps)
    return lax.ppermute(value, AXES, [(at, at + steps) for at in range(initial, last)])


def local(query_in, key_in, value_in, conv_taps, long_filter, skip_gain, grad_out):
    rows, channels = query_in.shape
    blocks = lax.axis_size("inner") * lax.axis_size("outer")
    width = channels // blocks
    unit = 8 if width % 8 == 0 else width
    groups = width // unit
    code_in = Code(-7.0, 4.0, 16.0, 12.0)
    reach = math.ceil(math.log2(blocks * rows * 1.1 * 63.0 * 63.0))
    code_out = Code(-7.0, 4.0, 12.0, float(reach))
    params = pltpu.CompilerParams(vmem_limit_bytes=VMEM_LIMIT)
    taps = conv_taps.reshape(9, channels)
    skip = skip_gain.reshape(1, channels)
    held_shape = (channels, rows) if groups == 1 else (blocks, width, rows)

    rim = jnp.concatenate([query_in[rows - 2 :], key_in[rows - 2 :], value_in[rows - 2 :]], axis=0)
    earlier = from_behind(rim, 1)
    packed = pl.pallas_call(
        functools.partial(gate_kernel, code_in, groups),
        out_shape=jax.ShapeDtypeStruct((3, channels, rows), bf16),
        scratch_shapes=[pltpu.VMEM((3,) + held_shape, f32)],
        compiler_params=params,
        name="gate",
    )(query_in, key_in, value_in, grad_out, long_filter, earlier, taps)
    spread = lax.all_to_all(packed.reshape(3, blocks, width, rows), AXES, 1, 1, tiled=True)
    result = pl.pallas_call(
        functools.partial(transform_kernel, code_in, code_out, groups),
        out_shape=jax.ShapeDtypeStruct((2, channels, rows), bf16),
        scratch_shapes=[pltpu.VMEM((3,) + held_shape, f32), pltpu.VMEM((2,) + held_shape, f32)],
        compiler_params=params,
        name="transform",
    )(spread.reshape(3, channels, rows), *[jnp.asarray(t) for t in tables(blocks, rows, unit)])
    returned = lax.all_to_all(result.reshape(2, blocks, width, rows), AXES, 1, 1, tiled=True)
    wide = jax.ShapeDtypeStruct((rows, channels), bf16)
    narrow = jax.ShapeDtypeStruct((6, channels), f32)
    output, grad_q, grad_k, grad_v, first, last = pl.pallas_call(
        functools.partial(finish_kernel, code_out, groups),
        out_shape=(wide, wide, wide, wide, narrow, narrow),
        scratch_shapes=[pltpu.VMEM((2,) + held_shape, f32)],
        compiler_params=params,
        name="finish",
    )(
        returned.reshape(2, channels, rows),
        query_in,
        key_in,
        value_in,
        grad_out,
        earlier,
        taps,
        skip,
    )
    later = from_behind(first, -1)
    tail = pl.BlockSpec((16, channels), lambda step: (rows // 16 - 1, 0))
    whole = [pl.BlockSpec((size, channels), lambda step: (0, 0)) for size in (6, 6, 9)]
    grad_q, grad_k, grad_v = pl.pallas_call(
        rim_kernel,
        grid=(1,),
        out_shape=(wide, wide, wide),
        in_specs=[tail, tail, tail] + whole,
        out_specs=(tail, tail, tail),
        input_output_aliases={0: 0, 1: 1, 2: 2},
        compiler_params=params,
        name="rim",
    )(grad_q, grad_k, grad_v, last, later, taps)
    return output, grad_q, grad_k, grad_v


def solution(mesh):
    split = P(AXES, None)
    return jax.shard_map(
        local,
        mesh=mesh,
        in_specs=(split, split, split, P(), split, P(), split),
        out_specs=(split, split, split, split),
        check_vma=False,
    )
```

profile of v0, /device:TPU:7, one launch (start us, length us, event | category | flops | bytes accessed | tf_op | source)
XLA Modules:
  0.0 83.6 jit_solution(8382903392050635371)
XLA Ops:
  0.6 0.0 copy-start.1
  0.6 0.7 slice.9
  1.4 0.7 slice.10
  2.1 0.7 slice.11
  2.8 3.7 %collective-permute-start = (bf16[6,1024]{1,0:T(8,128)(2,1)S(1)}, bf16[6,1024]{1,0:T(8,128)(2,1)S(1)}, u32[]{:S(2)}, u32[]{:S(2)}) collective-permute-start(bf16[6,1024]{1,0:T(8,128)(2,1)S(1)} %pad_maximum_fusion), channel_id=1, source_target_pairs={{0,1},{1,2},{2,3},{3,4},{4,5},{5,6},{6,7},{7,8},{8,9},{9,10},{10,1... | collective-permute-start | bytes 36872 | tf_op jit(solution)/shard_map/ppermute | solution.py:276
  6.5 0.0 copy-done.1
  6.5 0.6 reshape.26.taps_ref
  7.2 0.2 collective-permute-done.rim_ref
  7.4 0.0 copy-start
  7.4 0.6 copy-done
  8.0 3.6 %gate.1 = bf16[3,1024,128]{2,1,0:T(8,128)(2,1)} custom-call(bf16[128,1024]{1,0:T(8,128)(2,1)} %q_ref.3, bf16[128,1024]{1,0:T(8,128)(2,1)} %k_ref.3, bf16[128,1024]{1,0:T(8,128)(2,1)} %v_ref.3, bf16[128,1024]{1,0:T(8,128)(2,1)} %g_ref.3, f32[128,1024]{1,0:T(8,128)} %h_ref.1, bf16[6,1024]{1,0:T(8,128)(2,1)} %copy-done, f32[9,1024]{1,0:T(8,128)} %reshape.26.taps_ref), custom_call_target="tpu_custom_call" | custom-call | tf_op jit(solution)/shard_map/gate/pallas_call | solution.py:295
  11.6 1.2 %copy.24 = bf16[3,32,32,128]{3,2,0,1:T(8,128)(2,1)S(1)} copy(bf16[3,32,32,128]{3,2,1,0:T(8,128)(2,1)} %bitcast.6) | data formatting | bytes 1572864 | tf_op jit(solution)/shard_map/reshape | solution.py:302
  12.8 26.5 %all_to_all.10 = bf16[3,32,32,128]{3,2,0,1:T(8,128)(2,1)S(1)} all-to-all(bf16[3,32,32,128]{3,2,0,1:T(8,128)(2,1)S(1)} %copy.24), channel_id=1, replica_groups=mesh['outer'=8,'inner'=4] {'outer','inner'}, dimensions={1} | all-to-all | bytes 1572864 | tf_op jit(solution)/shard_map/all_to_all | solution.py:302
  39.3 1.0 %copy.25 = bf16[3,32,32,128]{3,2,1,0:T(8,128)(2,1)} copy(bf16[3,32,32,128]{3,2,0,1:T(8,128)(2,1)S(1)} %all_to_all.10) | data formatting | bytes 1572864 | tf_op jit(solution)/shard_map/all_to_all | solution.py:302
  40.2 9.4 %transform.1 = bf16[2,1024,128]{2,1,0:T(8,128)(2,1)} custom-call(bf16[3,1024,128]{2,1,0:T(8,128)(2,1)} %bitcast.5, bf16[512,256]{1,0:T(8,128)(2,1)} %constant.20.clone.refs_1_, bf16[512,256]{1,0:T(8,128)(2,1)} %constant.21.clone.refs_2_, bf16[256,512]{1,0:T(8,128)(2,1)} %constant.22.clone.refs_3_, bf16[256,512]{1,0:T(8,128)(2,1)} %constant.23.clone.refs_4_, ...), custom_call_target="tpu_custom_call" | custom-call | tf_op jit(solution)/shard_map/transform/pallas_call | solution.py:303
  49.7 1.1 %copy.26 = bf16[2,32,32,128]{3,2,0,1:T(8,128)(2,1)S(1)} copy(bf16[2,32,32,128]{3,2,1,0:T(8,128)(2,1)} %bitcast.8) | data formatting | bytes 1048576 | tf_op jit(solution)/shard_map/reshape | solution.py:310
  50.8 18.5 %all_to_all.11 = bf16[2,32,32,128]{3,2,0,1:T(8,128)(2,1)S(1)} all-to-all(bf16[2,32,32,128]{3,2,0,1:T(8,128)(2,1)S(1)} %copy.26), channel_id=1, replica_groups=mesh['outer'=8,'inner'=4] {'outer','inner'}, dimensions={1} | all-to-all | bytes 1048576 | tf_op jit(solution)/shard_map/all_to_all | solution.py:310
  69.3 0.8 copy.27
  70.1 4.1 %finish.1 = (bf16[128,1024]{1,0:T(8,128)(2,1)}, bf16[128,1024]{1,0:T(8,128)(2,1)}, bf16[128,1024]{1,0:T(8,128)(2,1)}, bf16[128,1024]{1,0:T(8,128)(2,1)}, f32[6,1024]{1,0:T(8,128)}, /*index=5*/f32[6,1024]{1,0:T(8,128)}) custom-call(bf16[2,1024,128]{2,1,0:T(8,128)(2,1)} %bitcast.7, bf16[128,1024]{1,0:T(8,128)(2,1)} %q_ref.3, bf16[128,1024]{1,0:T(8,128)(2,1)} %k_ref.3, ...), custom_call_target="tpu_custom_call" | custom-call | tf_op jit(solution)/shard_map/finish/pallas_call | solution.py:313
  74.2 2.8 %collective-permute-start.1 = (f32[6,1024]{1,0:T(8,128)}, f32[6,1024]{1,0:T(8,128)S(1)}, u32[]{:S(2)}, u32[]{:S(2)}) collective-permute-start(f32[6,1024]{1,0:T(8,128)} %get-tuple-element.18), channel_id=1, source_target_pairs={{1,0},{2,1},{3,2},{4,3},{5,4},{6,5},{7,6},{8,7},{9,8},{10,9},{11,1... | collective-permute-start | bytes 73736 | tf_op jit(solution)/shard_map/ppermute | solution.py:276
  77.0 4.4 %collective-permute-done.1.later_ref = f32[6,1024]{1,0:T(8,128)S(1)} collective-permute-done((f32[6,1024]{1,0:T(8,128)}, f32[6,1024]{1,0:T(8,128)S(1)}, u32[]{:S(2)}, u32[]{:S(2)}) %collective-permute-start.1) | collective-permute-done | bytes 24608 | tf_op jit(solution)/shard_map/ppermute | solution.py:276
  81.4 0.0 copy-start.2
  81.4 0.6 copy-done.2
  82.1 1.6 %rim.1 = (bf16[128,1024]{1,0:T(8,128)(2,1)}, bf16[128,1024]{1,0:T(8,128)(2,1)}, bf16[128,1024]{1,0:T(8,128)(2,1)}) custom-call(bf16[128,1024]{1,0:T(8,128)(2,1)} %get-tuple-element.14.gq_ref, bf16[128,1024]{1,0:T(8,128)(2,1)} %get-tuple-element.15.gk_ref, ...), custom_call_target="tpu_custom_call", output_to_operand_aliasing={{0}: (0, {}), {1}: (1, {}), {2}: (2, {})} | custom-call | tf_op jit(solution)/shard_map/rim/pallas_call | solution.py:332
  (1 shorter events, 0.0 us)
Async XLA Ops:
  0.6 5.9 %copy-start.1 = (f32[3,3,1024]{2,1,0:T(4,128)S(1)}, f32[3,3,1024]{2,1,0:T(4,128)}, u32[]{:S(2)}) copy-start(f32[3,3,1024]{2,1,0:T(4,128)} %param.20) | copy-start | bytes 110596
  2.8 4.5 %collective-permute-start = (bf16[6,1024]{1,0:T(8,128)(2,1)S(1)}, bf16[6,1024]{1,0:T(8,128)(2,1)S(1)}, u32[]{:S(2)}, u32[]{:S(2)}) collective-permute-start(bf16[6,1024]{1,0:T(8,128)(2,1)S(1)} %pad_maximum_fusion), channel_id=1, source_target_pairs={{0,1},{1,2},{2,3},{3,4},{4,5},{5,6},{6,7},{7,8},{8,9},{9,10},{10,1... | collective-permute-start | bytes 36872 | tf_op jit(solution)/shard_map/ppermute | solution.py:276
  7.4 0.6 copy-start
  74.2 7.2 %collective-permute-start.1 = (f32[6,1024]{1,0:T(8,128)}, f32[6,1024]{1,0:T(8,128)S(1)}, u32[]{:S(2)}, u32[]{:S(2)}) collective-permute-start(f32[6,1024]{1,0:T(8,128)} %get-tuple-element.18), channel_id=1, source_target_pairs={{1,0},{2,1},{3,2},{4,3},{5,4},{6,5},{7,6},{8,7},{9,8},{10,9},{11,1... | collective-permute-start | bytes 73736 | tf_op jit(solution)/shard_map/ppermute | solution.py:276
  81.4 0.6 copy-start.2
where the time goes:
time: 84.2 us; the launch traced here: 83.6 us
  blocking collectives  45 us (53%)
  Pallas kernels  18.8 us (22%)
  local copies, waits for them, and re-layouts  8.13 us (10%)
  starting transfers between devices  6.46 us (8%)
  waiting for transfers between devices  4.64 us (6%)
    all_to_all x1, blocking collectives, local(): lax.all_to_all(packed.reshape(3, blocks, width, rows), AXES, 1, 1, tiled=...  26.5 us
    all_to_all x1, blocking collectives, local(): lax.all_to_all(result.reshape(2, blocks, width, rows), AXES, 1, 1, tiled=...  18.5 us
    pallas_call x1, Pallas kernels, local(): pl.pallas_call(functools.partial(transform_kernel, code_in, code_out, gro...  9.43 us
    ppermute x2, starting transfers between devices, from_behind(): lax.ppermute(value, AXES, [(at, at + steps) for at in range(initial, last)])  6.46 us
    ppermute x2, waiting for transfers between devices, from_behind(): lax.ppermute(value, AXES, [(at, at + steps) for at in range(initial, last)])  4.64 us
    pallas_call x1, Pallas kernels, local(): pl.pallas_call(functools.partial(finish_kernel, code_out, groups), out_sh...  4.11 us
    pallas_call x1, Pallas kernels, local(): pl.pallas_call(functools.partial(gate_kernel, code_in, groups), out_shape...  3.63 us
  transfers between devices with their start and end apart: 2, of which 2 were waited for; matrix products, arithmetic and copies ran while one was open for 1% of the time, Pallas kernels for 0%

commit v1 on v0

v1 whole, which is shorter than its diff:
```python
import functools
import math

import jax
import jax.numpy as jnp
import ml_dtypes
import numpy as np
from jax import lax
from jax.experimental import pallas as pl
from jax.experimental.pallas import tpu as pltpu
from jax.sharding import PartitionSpec as P

AXES = ("outer", "inner")
f32 = jnp.float32
bf16 = jnp.bfloat16
ITEMS = 32

LOW, HIGH, STEEP, FLAT = -11.0, 0.25, 17.0, 4.0
AT_HIGH = 126.0
AT_LOW = AT_HIGH - STEEP * (HIGH - LOW)


def encode(value):
    place = jnp.log2(jnp.abs(value))
    inside = jnp.clip(place, LOW, HIGH)
    size = jnp.exp2(FLAT * place + ((STEEP - FLAT) * inside + (AT_HIGH - STEEP * HIGH)))
    return jnp.where(value < 0, -size, size)


def decode(word):
    code = jnp.log2(jnp.abs(word))
    inside = jnp.clip(code, AT_LOW, AT_HIGH)
    size = jnp.exp2(
        (1.0 / FLAT) * code + ((1.0 / STEEP - 1.0 / FLAT) * inside + (HIGH - AT_HIGH / STEEP))
    )
    return jnp.where(word < 0, -size, size)


def scale_of(peaks):
    top = jnp.max(jnp.max(peaks, axis=0, keepdims=True), axis=1, keepdims=True)
    return jnp.maximum(top, 2.0**-100).astype(bf16).astype(f32)


def peaks_of(value):
    rows, lanes = value.shape
    return jnp.max(jnp.abs(value).reshape(rows // 8, 8, lanes), axis=0)


def split_pair(value):
    high = value.astype(bf16)
    return high, (value - high.astype(f32)).astype(bf16)


def numpy_pair(value):
    high = value.astype(np.float32).astype(ml_dtypes.bfloat16)
    low = (value - high.astype(np.float64)).astype(np.float32).astype(ml_dtypes.bfloat16)
    return high, low


def table_on_left(table, value):
    high, low = split_pair(value)
    return jnp.dot(table, jnp.concatenate([high, low, high], axis=0), preferred_element_type=f32)


def table_on_right(value, table):
    high, low = split_pair(value)
    return jnp.dot(jnp.concatenate([high, high, low], axis=1), table, preferred_element_type=f32)


@functools.lru_cache(maxsize=None)
def tables(blocks, rows, unit):
    points = 2 * blocks * rows
    bins = np.arange(blocks) + 0.5
    angle = np.outer(bins, np.arange(blocks)) * (2 * math.pi / (2 * blocks))
    eye = np.eye(unit)
    coarse = np.concatenate([np.kron(np.cos(angle), eye), np.kron(-np.sin(angle), eye)], axis=0)
    coarse_back = np.concatenate(
        [np.kron(np.cos(angle).T, eye), np.kron(-np.sin(angle).T, eye)], axis=1
    ) * (2.0 / points)
    twist = np.repeat(np.outer(bins, np.arange(rows)) * (2 * math.pi / points), unit, axis=0)
    fine = np.outer(np.arange(rows), np.arange(rows)) * (2 * math.pi / rows)
    cos, sin = np.cos(fine), np.sin(fine)
    forward = np.block([[cos, -sin], [sin, cos]])
    backward = np.block([[cos, sin], [-sin, cos]])
    flat = []
    for table in (coarse, coarse_back):
        high, low = numpy_pair(table)
        flat.append(np.concatenate([high, high, low], axis=1))
    for table in (forward, backward):
        high, low = numpy_pair(table)
        flat.append(np.concatenate([high, low, high], axis=0))
    return flat + [np.cos(twist).astype(np.float32), np.sin(twist).astype(np.float32)]


def shifted(stream, steps, rim):
    rolled = pltpu.roll(stream, steps, 0)
    if rim is None:
        return rolled
    row = lax.broadcasted_iota(jnp.int32, stream.shape, 0)
    if steps == 1:
        return jnp.where(row == 0, rim[1:2], rolled)
    return jnp.where(row == 0, rim[0:1], jnp.where(row == 1, rim[1:2], rolled))


def short_forward(stream, taps, which, rim):
    at = 3 * which
    return (
        taps[at : at + 1] * stream
        + taps[at + 1 : at + 2] * shifted(stream, 1, rim)
        + taps[at + 2 : at + 3] * shifted(stream, 2, rim)
    )


def short_after(stream, following, taps, which):
    at, rows = 3 * which, stream.shape[0]
    window = jnp.concatenate([stream[rows - 2 :], following], axis=0)
    return (
        taps[at : at + 1] * window[2:4]
        + taps[at + 1 : at + 2] * window[1:3]
        + taps[at + 2 : at + 3] * window[0:2]
    )


def ahead(rows, steps, rim):
    count = rows.shape[0]
    rolled = pltpu.roll(rows, count - steps, 0)
    row = lax.broadcasted_iota(jnp.int32, rows.shape, 0)
    if steps == 1:
        return jnp.where(row == count - 1, rim[0:1], rolled)
    return jnp.where(row == count - 2, rim[0:1], jnp.where(row == count - 1, rim[1:2], rolled))


def gate_kernel(groups, q_ref, k_ref, v_ref, g_ref, h_ref, taps_ref, out_ref, held, extra):
    rows, channels = q_ref.shape
    blocks = out_ref.shape[0]
    count = channels // groups
    unit = count // blocks
    width = unit * groups
    chunk = min(128, count)
    peaks = [None, None, None]
    extra[...] = jnp.zeros(extra.shape, f32)
    for start in range(0, channels, chunk):
        lanes = pl.ds(start, chunk)
        group, first = start // count, start % count // unit
        taps = taps_ref[:, lanes]
        query, key = q_ref[:, lanes].astype(f32), k_ref[:, lanes].astype(f32)
        value, upstream = v_ref[:, lanes].astype(f32), g_ref[:, lanes].astype(f32)
        for at, stream in enumerate((key, value, query, upstream)):
            extra[2 * at : 2 * at + 2, lanes] = stream[0:2]
        for at, stream in enumerate((key, value, query)):
            extra[8 + 2 * at : 10 + 2 * at, lanes] = stream[rows - 2 :]
        short_q = short_forward(query, taps, 0, None)
        short_k = short_forward(key, taps, 1, None)
        short_v = short_forward(value, taps, 2, None)
        for which, signal in enumerate((short_k * short_v, h_ref[:, lanes], upstream * short_q)):
            peak = peaks_of(signal)
            peaks[which] = peak if peaks[which] is None else jnp.maximum(peaks[which], peak)
            held[
                pl.ds(first, chunk // unit), pl.ds(which * width + group * unit, unit), :
            ] = signal.T.reshape(chunk // unit, unit, rows)
    for which in range(3):
        scale = scale_of(peaks[which])
        extra[14 + which : 15 + which, :] = jnp.broadcast_to(scale, (1, channels))
        part = pl.ds(which * width, width)
        out_ref[:, part, :] = encode(held[:, part, :] * (1.0 / scale)).astype(bf16)
    items = [extra[:, group * count : (group + 1) * count] for group in range(groups)]
    if ITEMS * groups < rows:
        items.append(jnp.zeros((rows - ITEMS * groups, count), f32))
    lines = jnp.concatenate(items, axis=0).T.reshape(blocks, unit, rows)
    out_ref[:, 3 * width :, :] = lines.astype(bf16)


def transform_kernel(groups, x_ref, own_ref, *refs):
    coarse_ref, coarse_back_ref, forward_ref, backward_ref, cos_ref, sin_ref = refs[:6]
    out_ref, held, back = refs[6:]
    blocks, lines, rows = x_ref.shape
    width = back.shape[1] // 2
    unit = width // groups
    count = blocks * unit
    held[...] = x_ref[...].astype(f32)

    extra = held[:, 3 * width :, :].reshape(count, rows)
    none = jnp.zeros((unit, rows), f32)
    before = jnp.concatenate([none, extra[: count - unit]], axis=0)
    after = jnp.concatenate([extra[unit:], none], axis=0)
    lane = lax.broadcasted_iota(jnp.int32, (count, rows), 1)
    item = lane % ITEMS

    def turn(value, steps):
        return value if steps % rows == 0 else pltpu.roll(value, steps % rows, 1)

    def own(tap):
        return jnp.broadcast_to(own_ref[tap][None], (blocks, unit, rows)).reshape(count, rows)

    middle = jnp.where(item % 2 == 0, turn(before, -9), turn(extra, 1))
    shorts = own(0) * extra + own(1) * middle + own(2) * turn(before, -8)
    edge_gated = shorts * turn(shorts, -2)
    edge_mixed = shorts * turn(extra, -2)

    def take(which, group):
        part = held[:, pl.ds(which * width + group * unit, unit), :].reshape(count, rows)
        signal = decode(part) * extra[:, 14 + which : 15 + which]
        if which == 1:
            return signal
        edge = (
            turn(edge_gated, -ITEMS * group)
            if which == 0
            else turn(edge_mixed, -ITEMS * group - 4)
        )
        return jnp.where(lane < 2, edge, signal)

    peaks = [None, None]
    together = 2 if groups % 2 == 0 else 1
    for base in range(0, groups, together):
        cos, sin = cos_ref[...], sin_ref[...]
        members = range(base, base + together)
        stacked = jnp.concatenate([take(which, g) for g in members for which in range(3)], axis=1)
        first = table_on_left(coarse_ref[...], stacked)
        lasts = []
        for at in range(together):
            spectra = []
            for which in range(3):
                here = slice((3 * at + which) * rows, (3 * at + which + 1) * rows)
                real, imag = first[:count, here], first[count:, here]
                turned = jnp.concatenate(
                    [real * cos + imag * sin, imag * cos - real * sin], axis=1
                )
                spectrum = table_on_right(turned, forward_ref[...])
                spectra.append((spectrum[:, :rows], spectrum[:, rows:]))
            (gr, gi), (hr, hi), (mr, mi) = spectra
            for real, imag in (
                (gr * hr - gi * hi, gr * hi + gi * hr),
                (mr * hr + mi * hi, mi * hr - mr * hi),
            ):
                product = jnp.concatenate([real, imag], axis=1)
                plain = table_on_right(product, backward_ref[...])
                real, imag = plain[:, :rows], plain[:, rows:]
                lasts.append(
                    jnp.concatenate([real * cos - imag * sin, imag * cos + real * sin], axis=0)
                )
        result = table_on_left(coarse_back_ref[...], jnp.concatenate(lasts, axis=1))
        for at, group in enumerate(members):
            for which in range(2):
                here = slice((2 * at + which) * rows, (2 * at + which + 1) * rows)
                part = result[:, here]
                peak = peaks_of(part)
                peaks[which] = peak if peaks[which] is None else jnp.maximum(peaks[which], peak)
                back[:, pl.ds(which * width + group * unit, unit), :] = part.reshape(
                    blocks, unit, rows
                )
    placed = jnp.zeros((count, rows), f32)
    for which in range(2):
        scale = scale_of(peaks[which])
        part = pl.ds(which * width, width)
        words = encode(back[:, part, :] * (1.0 / scale))
        out_ref[:, part, :] = words.astype(bf16)
        for group in range(groups):
            mine = words[:, group * unit : (group + 1) * unit, :].reshape(count, rows)
            at = ITEMS * group + 16 + 2 * which
            placed = jnp.where((lane >= at) & (lane < at + 2), turn(mine, at), placed)
        placed = jnp.where(item == 20 + which, scale, placed)
    following = jnp.concatenate([placed[unit:], none], axis=0)
    placed = jnp.where(item < 20, following, placed)
    lines = jnp.where(item < 8, after, jnp.where(item < 14, before, placed))
    out_ref[:, 2 * width :, :] = lines.reshape(blocks, unit, rows).astype(bf16)


def finish_kernel(groups, y_ref, q_ref, k_ref, v_ref, g_ref, taps_ref, skip_ref, *refs):
    out_ref, gq_ref, gk_ref, gv_ref, held = refs
    rows, channels = q_ref.shape
    blocks = y_ref.shape[0]
    count = channels // groups
    unit = count // blocks
    width = unit * groups
    chunk = min(128, count)
    held[...] = y_ref[...].astype(f32)
    extra = held[:, 2 * width :, :].reshape(count, rows).T
    for start in range(0, channels, chunk):
        lanes = pl.ds(start, chunk)
        group, first = start // count, start % count // unit
        taps = taps_ref[:, lanes]
        skip = skip_ref[:, lanes]
        inner = start % count
        items = extra[ITEMS * group : ITEMS * (group + 1), inner : inner + chunk]
        after = [items[2 * at : 2 * at + 2] for at in range(4)]
        before = [items[8 + 2 * at : 10 + 2 * at] for at in range(3)]

        def arrived(which):
            part = held[
                pl.ds(first, chunk // unit), pl.ds(which * width + group * unit, unit), :
            ].reshape(chunk, rows)
            scale = items[20 + which : 21 + which]
            return decode(part).T * scale, decode(items[16 + 2 * which : 18 + 2 * which]) * scale

        query, key = q_ref[:, lanes].astype(f32), k_ref[:, lanes].astype(f32)
        value, upstream = v_ref[:, lanes].astype(f32), g_ref[:, lanes].astype(f32)
        shorts = [
            (
                short_forward(stream, taps, which, before[at]),
                short_after(stream, after[at], taps, which),
            )
            for which, at, stream in ((0, 2, query), (1, 0, key), (2, 1, value))
        ]
        results = (arrived(0), arrived(1))
        upstreams = (upstream, after[3])
        grads = [[], [], []]
        for here in range(2):
            short_q, short_k, short_v = (short[here] for short in shorts)
            mixed = results[0][here] + skip * (short_k * short_v)
            if here == 0:
                out_ref[:, lanes] = (short_q * mixed).astype(bf16)
            grad_gated = results[1][here] + skip * (upstreams[here] * short_q)
            grads[0].append(upstreams[here] * mixed)
            grads[1].append(grad_gated * short_v)
            grads[2].append(grad_gated * short_k)
        for which, ref in enumerate((gq_ref, gk_ref, gv_ref)):
            rows_of, rim = grads[which]
            at = 3 * which
            ref[:, lanes] = (
                taps[at : at + 1] * rows_of
                + taps[at + 1 : at + 2] * ahead(rows_of, 1, rim)
                + taps[at + 2 : at + 3] * ahead(rows_of, 2, rim)
            ).astype(bf16)


def local(query_in, key_in, value_in, conv_taps, long_filter, skip_gain, grad_out):
    rows, channels = query_in.shape
    blocks = lax.axis_size("inner") * lax.axis_size("outer")
    width = channels // blocks
    unit = 8 if width % 8 == 0 else width
    groups = width // unit
    params = pltpu.CompilerParams(vmem_limit_bytes=(24 if unit == 8 else 56) * 1024 * 1024)
    taps = conv_taps.reshape(9, channels)
    skip = skip_gain.reshape(1, channels)

    own = conv_taps.reshape(3, 3, groups, blocks, unit)
    own = lax.dynamic_index_in_dim(own, lax.axis_index(AXES), 3, keepdims=False)
    own = jnp.stack([own[1], own[2], own[0]])
    own = jnp.repeat(jnp.transpose(own, (1, 3, 2, 0)), 2, axis=3)
    own = jnp.pad(own, ((0, 0), (0, 0), (0, 0), (0, ITEMS - 6))).reshape(3, unit, ITEMS * groups)
    own = jnp.pad(own, ((0, 0), (0, 0), (0, rows - ITEMS * groups)))

    lines = 3 * width + unit
    packed = pl.pallas_call(
        functools.partial(gate_kernel, groups),
        out_shape=jax.ShapeDtypeStruct((blocks, lines, rows), bf16),
        scratch_shapes=[
            pltpu.VMEM((blocks, 3 * width, rows), f32),
            pltpu.VMEM((ITEMS, channels), f32),
        ],
        compiler_params=params,
        name="gate",
    )(query_in, key_in, value_in, grad_out, long_filter, taps)
    spread = lax.all_to_all(packed, AXES, 0, 0, tiled=True)
    lines_back = 2 * width + unit
    result = pl.pallas_call(
        functools.partial(transform_kernel, groups),
        out_shape=jax.ShapeDtypeStruct((blocks, lines_back, rows), bf16),
        scratch_shapes=[
            pltpu.VMEM((blocks, lines, rows), f32),
            pltpu.VMEM((blocks, 2 * width, rows), f32),
        ],
        compiler_params=params,
        name="transform",
    )(spread, own, *[jnp.asarray(table) for table in tables(blocks, rows, unit)])
    returned = lax.all_to_all(result, AXES, 0, 0, tiled=True)
    wide = jax.ShapeDtypeStruct((rows, channels), bf16)
    return pl.pallas_call(
        functools.partial(finish_kernel, groups),
        out_shape=(wide, wide, wide, wide),
        scratch_shapes=[pltpu.VMEM((blocks, lines_back, rows), f32)],
        compiler_params=params,
        name="finish",
    )(returned, query_in, key_in, value_in, grad_out, taps, skip)


def solution(mesh):
    split = P(AXES, None)
    return jax.shard_map(
        local,
        mesh=mesh,
        in_specs=(split, split, split, P(), split, P(), split),
        out_specs=(split, split, split, split),
        check_vma=False,
    )
```

time: 84.2 us -> 68.2 us (0.81)
  the two profiles are of different devices: /device:TPU:7 before, /device:TPU:0 now
where the time goes in v1:
time: 68.2 us; the launch traced here: 67.6 us
  blocking collectives  20.2 us (30%)
  waiting for transfers between devices  15.4 us (23%)
  local copies, waits for them, and re-layouts  12.3 us (18%)
  Pallas kernels  11.6 us (17%)
  starting transfers between devices  7.3 us (11%)
  between operations  0.8 us (1%)
    all_to_all x1, blocking collectives, local(): returned = lax.all_to_all(result, AXES, 0, 0, tiled=True)  20.2 us
    all_to_all x1, waiting for transfers between devices, local(): spread = lax.all_to_all(packed, AXES, 0, 0, tiled=True)  15.4 us
    all_to_all x1, starting transfers between devices, local(): spread = lax.all_to_all(packed, AXES, 0, 0, tiled=True)  7.3 us
    unnamed x35, local copies, waits for them, and re-layouts  6.46 us
    pallas_call x1, Pallas kernels, local(): pl.pallas_call(functools.partial(transform_kernel, groups), out_shape=jax...  6.29 us
    pallas_call x1, Pallas kernels, local(): pl.pallas_call(functools.partial(finish_kernel, groups), out_shape=(wide,...  2.97 us
    pallas_call x1, Pallas kernels, local(): pl.pallas_call(functools.partial(gate_kernel, groups), out_shape=jax.Shap...  2.35 us
    pad x1, local copies, waits for them, and re-layouts, local(): jnp.pad(own, ((0, 0), (0, 0), (0, 0), (0, ITEMS - 6)))  1.43 us
  transfers between devices with their start and end apart: 1, of which 1 were waited for; matrix products, arithmetic and copies ran while one was open for 10% of the time, Pallas kernels for 0%

profile of v1, /device:TPU:0, one launch (start us, length us, event | category | flops | bytes accessed | tf_op | source)
XLA Modules:
  0.0 67.6 jit_solution(13465175064537564385)
XLA Ops:
  0.6 0.8 %reshape.26.taps_ref = f32[9,1024]{1,0:T(8,128)S(1)} reshape(f32[3,3,1024]{2,1,0:T(4,128)} %param.16) | data formatting | bytes 73728 | tf_op jit(solution)/shard_map/reshape | solution.py:333
  1.5 0.0 copy-start
  1.5 0.9 %copy-done = bf16[128,1024]{1,0:T(8,128)(2,1)S(1)} copy-done((bf16[128,1024]{1,0:T(8,128)(2,1)S(1)}, bf16[128,1024]{1,0:T(8,128)(2,1)}, u32[]{:S(2)}) %copy-start) | copy-done | bytes 262168
  2.4 0.0 copy-start.2
  2.4 0.9 %copy-done.2 = bf16[128,1024]{1,0:T(8,128)(2,1)S(1)} copy-done((bf16[128,1024]{1,0:T(8,128)(2,1)S(1)}, bf16[128,1024]{1,0:T(8,128)(2,1)}, u32[]{:S(2)}) %copy-start.2) | copy-done | bytes 262168
  3.4 0.0 copy-start.4
  3.4 0.9 %copy-done.4 = bf16[128,1024]{1,0:T(8,128)(2,1)S(1)} copy-done((bf16[128,1024]{1,0:T(8,128)(2,1)S(1)}, bf16[128,1024]{1,0:T(8,128)(2,1)}, u32[]{:S(2)}) %copy-start.4) | copy-done | bytes 262168
  4.3 0.0 copy-start.6
  4.3 0.9 %copy-done.6 = bf16[128,1024]{1,0:T(8,128)(2,1)S(1)} copy-done((bf16[128,1024]{1,0:T(8,128)(2,1)S(1)}, bf16[128,1024]{1,0:T(8,128)(2,1)}, u32[]{:S(2)}) %copy-start.6) | copy-done | bytes 262168
  5.3 0.0 copy-start.10
  5.3 1.0 %copy-done.10 = f32[128,1024]{1,0:T(8,128)S(1)} copy-done((f32[128,1024]{1,0:T(8,128)S(1)}, f32[128,1024]{1,0:T(8,128)}, u32[]{:S(2)}) %copy-start.10) | copy-done | bytes 524312
  6.3 2.3 %gate.1 = bf16[32,104,128]{2,1,0:T(8,128)(2,1)} custom-call(bf16[128,1024]{1,0:T(8,128)(2,1)S(1)} %copy-done, bf16[128,1024]{1,0:T(8,128)(2,1)S(1)} %copy-done.2, bf16[128,1024]{1,0:T(8,128)(2,1)S(1)} %copy-done.4, bf16[128,1024]{1,0:T(8,128)(2,1)S(1)} %copy-done.6, f32[128,1024]{1,0:T(8,128)S(1)} %copy-done.10, f32[9,1024]{1,0:T(8,128)S(1)} %reshape.26.taps_ref), custom_call_target="tpu_custom_call" | custom-call | tf_op jit(solution)/shard_map/gate/pallas_call | solution.py:344
  8.6 0.0 copy-start.16
  8.6 0.0 copy-start.9
  8.7 0.0 copy-start.11
  8.7 0.0 copy-start.12
  8.7 7.3 %all-to-all-start = ((bf16[32,104,128]{2,1,0:T(8,128)(2,1)}), bf16[32,104,128]{2,1,0:T(8,128)(2,1)S(1)}, u32[]{:S(2)}, u32[]{:S(2)}) async-start(bf16[32,104,128]{2,1,0:T(8,128)(2,1)} %gate.1), calls=%async_computation | async-start | bytes 1703936 | tf_op jit(solution)/shard_map/all_to_all | solution.py:354
  16.0 0.0 copy-done.16
  16.0 0.0 copy-start.8
  16.0 1.2 %reshape.27 = f32[3,3,4,32,8]{4,3,2,1,0:T(8,128)} reshape(f32[3,3,1024]{2,1,0:T(4,128)S(1)} %copy-done.16) | data formatting | bytes 73728 | tf_op jit(solution)/shard_map/reshape | solution.py:336
  17.2 0.9 %constant_dynamic-slice_fusion.1 = (f32[1,3,4,1,8]{4,3,2,1,0:T(1,128)S(1)}, f32[1,3,4,1,8]{4,3,2,1,0:T(1,128)S(1)}, f32[1,3,4,1,8]{4,3,2,1,0:T(1,128)S(1)}) fusion(f32[3,3,4,32,8]{4,3,2,1,0:T(8,128)} %reshape.27, s32[]{:T(128)S(6)} %add.11, s32[]{:T(128)S(6)} %select_n.4, s32[]{:T(128)S(6)} %add.12), kind=kLoop, calls=%fused_computation.2 | loop fusion | bytes 2316 | tf_op jit(solution)/shard_map/slice | solution.py:338
  18.1 0.0 copy-start.14
  18.1 0.6 broadcast_in_dim.3
  18.7 0.0 copy-start.13
  18.7 1.6 %copy.21 = f32[3,8,4,6]{3,2,1,0:T(4,128)} copy(f32[3,8,4,6]{1,2,3,0:T(4,128)} %bitcast.8) | data formatting | bytes 4608
  20.3 1.4 %pad.4.clone = f32[3,8,4,32]{3,2,1,0:T(4,128)} pad(f32[3,8,4,6]{3,2,1,0:T(4,128)} %copy.21, f32[]{:T(128)} %constant.31.clone.1), padding=0_0x0_0x0_0x0_26 | pad | bytes 14596 | tf_op jit(solution)/shard_map/jit(_pad)/pad | solution.py:340
  21.7 0.9 %reshape.29.own_ref = f32[3,8,128]{2,1,0:T(8,128)S(1)} reshape(f32[3,8,4,32]{3,2,1,0:T(4,128)} %pad.4.clone) | data formatting | bytes 24576 | tf_op jit(solution)/shard_map/reshape | solution.py:340
  22.6 15.4 %all-to-all-done.x_ref = bf16[32,104,128]{2,1,0:T(8,128)(2,1)S(1)} async-done(((bf16[32,104,128]{2,1,0:T(8,128)(2,1)}), bf16[32,104,128]{2,1,0:T(8,128)(2,1)S(1)}, u32[]{:S(2)}, u32[]{:S(2)}) %all-to-all-start) | async-done | bytes 852000 | tf_op jit(solution)/shard_map/all_to_all | solution.py:354
  38.0 0.0 copy-done.9
  38.0 0.0 copy-done.11
  38.0 0.0 copy-done.12
  38.0 0.0 copy-done.8
  38.0 0.0 copy-done.14
  38.0 0.0 copy-done.13
  38.0 6.3 %transform.1 = bf16[32,72,128]{2,1,0:T(8,128)(2,1)S(1)} custom-call(bf16[32,104,128]{2,1,0:T(8,128)(2,1)S(1)} %all-to-all-done.x_ref, f32[3,8,128]{2,1,0:T(8,128)S(1)} %reshape.29.own_ref, bf16[512,768]{1,0:T(8,128)(2,1)S(1)} %copy-done.8, bf16[256,1536]{1,0:T(8,128)(2,1)S(1)} %copy-done.9, bf16[768,256]{1,0:T(8,128)(2,1)S(1)} %copy-done.11, ...), custom_call_target="tpu_custom_call" | custom-call | tf_op jit(solution)/shard_map/transform/pallas_call | solution.py:356
  44.3 0.0 copy-start.1
  44.3 0.0 copy-start.3
  44.4 0.0 copy-start.5
  44.4 0.0 copy-start.7
  44.4 0.0 copy-start.15
  44.4 20.2 %all_to_all.10.y_ref = bf16[32,72,128]{2,1,0:T(8,128)(2,1)S(1)} all-to-all(bf16[32,72,128]{2,1,0:T(8,128)(2,1)S(1)} %transform.1), channel_id=1, replica_groups=mesh['outer'=8,'inner'=4] {'outer','inner'}, dimensions={0} | all-to-all | bytes 1179648 | tf_op jit(solution)/shard_map/all_to_all | solution.py:366
  64.6 0.0 copy-done.1
  64.6 0.0 copy-done.3
  64.6 0.0 copy-done.5
  64.6 0.0 copy-done.7
  64.6 0.0 copy-done.15
  64.6 3.0 %finish.1 = (bf16[128,1024]{1,0:T(8,128)(2,1)}, bf16[128,1024]{1,0:T(8,128)(2,1)}, bf16[128,1024]{1,0:T(8,128)(2,1)}, bf16[128,1024]{1,0:T(8,128)(2,1)}) custom-call(bf16[32,72,128]{2,1,0:T(8,128)(2,1)S(1)} %all_to_all.10.y_ref, bf16[128,1024]{1,0:T(8,128)(2,1)S(1)} %copy-done.1, bf16[128,1024]{1,0:T(8,128)(2,1)S(1)} %copy-done.3, ...), custom_call_target="tpu_custom_call" | custom-call | tf_op jit(solution)/shard_map/finish/pallas_call | solution.py:368
  (2 shorter events, 0.0 us)
Async XLA Ops:
  1.5 1.0 %copy-start = (bf16[128,1024]{1,0:T(8,128)(2,1)S(1)}, bf16[128,1024]{1,0:T(8,128)(2,1)}, u32[]{:S(2)}) copy-start(bf16[128,1024]{1,0:T(8,128)(2,1)} %q_ref.3) | copy-start | bytes 786436
  2.4 0.9 %copy-start.2 = (bf16[128,1024]{1,0:T(8,128)(2,1)S(1)}, bf16[128,1024]{1,0:T(8,128)(2,1)}, u32[]{:S(2)}) copy-start(bf16[128,1024]{1,0:T(8,128)(2,1)} %k_ref.3) | copy-start | bytes 786436
  3.4 0.9 %copy-start.4 = (bf16[128,1024]{1,0:T(8,128)(2,1)S(1)}, bf16[128,1024]{1,0:T(8,128)(2,1)}, u32[]{:S(2)}) copy-start(bf16[128,1024]{1,0:T(8,128)(2,1)} %v_ref.3) | copy-start | bytes 786436
  4.3 0.9 %copy-start.6 = (bf16[128,1024]{1,0:T(8,128)(2,1)S(1)}, bf16[128,1024]{1,0:T(8,128)(2,1)}, u32[]{:S(2)}) copy-start(bf16[128,1024]{1,0:T(8,128)(2,1)} %g_ref.3) | copy-start | bytes 786436
  5.3 1.0 %copy-start.10 = (f32[128,1024]{1,0:T(8,128)S(1)}, f32[128,1024]{1,0:T(8,128)}, u32[]{:S(2)}) copy-start(f32[128,1024]{1,0:T(8,128)} %h_ref.1) | copy-start | bytes 1572868
  8.6 7.3 %copy-start.16 = (f32[3,3,1024]{2,1,0:T(4,128)S(1)}, f32[3,3,1024]{2,1,0:T(4,128)}, u32[]{:S(2)}) copy-start(f32[3,3,1024]{2,1,0:T(4,128)} %param.16) | copy-start | bytes 110596
  8.6 29.3 %copy-start.9 = (bf16[256,1536]{1,0:T(8,128)(2,1)S(1)}, bf16[256,1536]{1,0:T(8,128)(2,1)}, u32[]{:S(2)}) copy-start(bf16[256,1536]{1,0:T(8,128)(2,1)} %constant.33.clone.refs_1_) | copy-start | bytes 2359300
  8.7 29.3 %copy-start.11 = (bf16[768,256]{1,0:T(8,128)(2,1)S(1)}, bf16[768,256]{1,0:T(8,128)(2,1)}, u32[]{:S(2)}) copy-start(bf16[768,256]{1,0:T(8,128)(2,1)} %constant.34.clone.refs_2_) | copy-start | bytes 1179652
  8.7 29.3 %copy-start.12 = (bf16[768,256]{1,0:T(8,128)(2,1)S(1)}, bf16[768,256]{1,0:T(8,128)(2,1)}, u32[]{:S(2)}) copy-start(bf16[768,256]{1,0:T(8,128)(2,1)} %constant.35.clone.refs_3_) | copy-start | bytes 1179652
  8.7 29.3 %all-to-all-start = ((bf16[32,104,128]{2,1,0:T(8,128)(2,1)}), bf16[32,104,128]{2,1,0:T(8,128)(2,1)S(1)}, u32[]{:S(2)}, u32[]{:S(2)}) async-start(bf16[32,104,128]{2,1,0:T(8,128)(2,1)} %gate.1), calls=%async_computation | async-start | bytes 1703936 | tf_op jit(solution)/shard_map/all_to_all | solution.py:354
  16.0 22.0 %copy-start.8 = (bf16[512,768]{1,0:T(8,128)(2,1)S(1)}, bf16[512,768]{1,0:T(8,128)(2,1)}, u32[]{:S(2)}) copy-start(bf16[512,768]{1,0:T(8,128)(2,1)} %constant.32.clone.refs_0_) | copy-start | bytes 2359300
  18.1 19.9 %copy-start.14 = (f32[256,128]{1,0:T(8,128)S(1)}, f32[256,128]{1,0:T(8,128)}, u32[]{:S(2)}) copy-start(f32[256,128]{1,0:T(8,128)} %constant.37.clone.refs_5_) | copy-start | bytes 393220
  18.7 19.3 %copy-start.13 = (f32[256,128]{1,0:T(8,128)S(1)}, f32[256,128]{1,0:T(8,128)}, u32[]{:S(2)}) copy-start(f32[256,128]{1,0:T(8,128)} %constant.36.clone.refs_4_) | copy-start | bytes 393220
  44.3 20.2 %copy-start.1 = (bf16[128,1024]{1,0:T(8,128)(2,1)S(1)}, bf16[128,1024]{1,0:T(8,128)(2,1)}, u32[]{:S(2)}) copy-start(bf16[128,1024]{1,0:T(8,128)(2,1)} %q_ref.3) | copy-start | bytes 786436
  44.3 20.2 %copy-start.3 = (bf16[128,1024]{1,0:T(8,128)(2,1)S(1)}, bf16[128,1024]{1,0:T(8,128)(2,1)}, u32[]{:S(2)}) copy-start(bf16[128,1024]{1,0:T(8,128)(2,1)} %k_ref.3) | copy-start | bytes 786436
  44.4 20.2 %copy-start.5 = (bf16[128,1024]{1,0:T(8,128)(2,1)S(1)}, bf16[128,1024]{1,0:T(8,128)(2,1)}, u32[]{:S(2)}) copy-start(bf16[128,1024]{1,0:T(8,128)(2,1)} %v_ref.3) | copy-start | bytes 786436
  44.4 20.2 %copy-start.7 = (bf16[128,1024]{1,0:T(8,128)(2,1)S(1)}, bf16[128,1024]{1,0:T(8,128)(2,1)}, u32[]{:S(2)}) copy-start(bf16[128,1024]{1,0:T(8,128)(2,1)} %g_ref.3) | copy-start | bytes 786436
  44.4 20.2 %copy-start.15 = (f32[1024]{0:T(1024)S(1)}, f32[1024]{0:T(1024)}, u32[]{:S(2)}) copy-start(f32[1024]{0:T(1024)} %param.18) | copy-start | bytes 12292

commit v2 on v1

v2 whole, which is shorter than its diff:
```python
import functools
import math

import jax
import jax.numpy as jnp
import ml_dtypes
import numpy as np
from jax import lax
from jax.experimental import pallas as pl
from jax.experimental.pallas import tpu as pltpu
from jax.sharding import PartitionSpec as P

AXES = ("outer", "inner")
f32 = jnp.float32
bf16 = jnp.bfloat16
ITEMS = 32

REACH = 240.0


def scale_of(top):
    return jnp.maximum(top, 2.0**-100).astype(bf16).astype(f32)


def encode(value, scale):
    power = value * (REACH / scale)
    sign = power < 0
    for _ in range(4):
        power = power * power
    return jnp.where(sign, -power, power)


def decode(word):
    size = jnp.exp2(jnp.log2(jnp.abs(word)) * (1.0 / 16.0))
    return jnp.where(word < 0, -size, size)


def split_pair(value):
    high = value.astype(bf16)
    return high, (value - high.astype(f32)).astype(bf16)


def numpy_pair(value):
    high = value.astype(np.float32).astype(ml_dtypes.bfloat16)
    low = (value - high.astype(np.float64)).astype(np.float32).astype(ml_dtypes.bfloat16)
    return high, low


def table_on_left(high_ref, low_ref, value):
    high, low = split_pair(value)
    table = jnp.concatenate([high_ref[...], high_ref[...], low_ref[...]], axis=1)
    return jnp.dot(table, jnp.concatenate([high, low, high], axis=0), preferred_element_type=f32)


def table_on_right(value, high_ref, low_ref):
    high, low = split_pair(value)
    table = jnp.concatenate([high_ref[...], low_ref[...], high_ref[...]], axis=0)
    return jnp.dot(jnp.concatenate([high, high, low], axis=1), table, preferred_element_type=f32)


@functools.lru_cache(maxsize=None)
def tables(blocks, rows, unit):
    points = 2 * blocks * rows
    bins = np.arange(blocks) + 0.5
    angle = np.outer(bins, np.arange(blocks)) * (2 * math.pi / (2 * blocks))
    eye = np.eye(unit)
    coarse = np.concatenate([np.kron(np.cos(angle), eye), np.kron(-np.sin(angle), eye)], axis=0)
    coarse_back = np.concatenate(
        [np.kron(np.cos(angle).T, eye), np.kron(-np.sin(angle).T, eye)], axis=1
    ) * (2.0 / points)
    twist = np.repeat(np.outer(bins, np.arange(rows)) * (2 * math.pi / points), unit, axis=0)
    fine = np.outer(np.arange(rows), np.arange(rows)) * (2 * math.pi / rows)
    cos, sin = np.cos(fine), np.sin(fine)
    forward = np.block([[cos, -sin], [sin, cos]])
    backward = np.block([[cos, sin], [-sin, cos]])
    flat = [half for table in (coarse, coarse_back, forward, backward) for half in numpy_pair(table)]
    return flat + [np.cos(twist).astype(np.float32), np.sin(twist).astype(np.float32)]


def shifted(stream, steps, rim):
    rolled = pltpu.roll(stream, steps, 0)
    if rim is None:
        return rolled
    row = lax.broadcasted_iota(jnp.int32, stream.shape, 0)
    if steps == 1:
        return jnp.where(row == 0, rim[1:2], rolled)
    return jnp.where(row == 0, rim[0:1], jnp.where(row == 1, rim[1:2], rolled))


def short_forward(stream, taps, rim):
    return taps[0] * stream + taps[1] * shifted(stream, 1, rim) + taps[2] * shifted(stream, 2, rim)


def short_after(stream, following, taps):
    window = jnp.concatenate([stream[stream.shape[0] - 2 :], following], axis=0)
    return taps[0] * window[2:4] + taps[1] * window[1:3] + taps[2] * window[0:2]


def taps_at(taps_ref, which, lanes):
    return [taps_ref[which, tap : tap + 1, lanes] for tap in range(3)]


def ahead(rows, steps, rim):
    count = rows.shape[0]
    rolled = pltpu.roll(rows, count - steps, 0)
    row = lax.broadcasted_iota(jnp.int32, rows.shape, 0)
    if steps == 1:
        return jnp.where(row == count - 1, rim[0:1], rolled)
    return jnp.where(row == count - 2, rim[0:1], jnp.where(row == count - 1, rim[1:2], rolled))


def gate_kernel(groups, q_ref, k_ref, v_ref, g_ref, h_ref, taps_ref, out_ref, extra):
    rows, channels = q_ref.shape
    blocks = out_ref.shape[0]
    count = channels // groups
    unit = count // blocks
    width = unit * groups
    chunk = min(128, count)
    together = 2 if groups % 2 == 0 else 1
    extra[14:ITEMS, :] = jnp.zeros((ITEMS - 14, channels), f32)

    def words(start):
        lanes = pl.ds(start, chunk)
        query, key = q_ref[:, lanes].astype(f32), k_ref[:, lanes].astype(f32)
        value, upstream = v_ref[:, lanes].astype(f32), g_ref[:, lanes].astype(f32)
        for at, stream in enumerate((key, value, query, upstream)):
            extra[2 * at : 2 * at + 2, lanes] = stream[0:2]
        for at, stream in enumerate((key, value, query)):
            extra[8 + 2 * at : 10 + 2 * at, lanes] = stream[rows - 2 :]
        short_q = short_forward(query, taps_at(taps_ref, 0, lanes), None)
        short_k = short_forward(key, taps_at(taps_ref, 1, lanes), None)
        short_v = short_forward(value, taps_at(taps_ref, 2, lanes), None)
        result = []
        row = lax.broadcasted_iota(jnp.int32, (8, chunk), 0)
        for which, signal in enumerate((short_k * short_v, h_ref[:, lanes], upstream * short_q)):
            if which != 1:
                edge = jnp.where(row < 2, 0.0, signal[:8])
                signal = jnp.concatenate([edge, signal[8:]], axis=0)
            scale = scale_of(jnp.max(jnp.abs(signal), axis=0, keepdims=True))
            extra[14 + which : 15 + which, lanes] = scale
            result.append(encode(signal, scale).T.reshape(chunk // unit, unit, rows))
        return result

    for base in range(0, groups, together):
        for inner in range(0, count, chunk):
            pieces = [words((base + at) * count + inner) for at in range(together)]
            for which in range(3):
                piece = jnp.concatenate([part[which] for part in pieces], axis=1)
                out_ref[
                    pl.ds(inner // unit, chunk // unit),
                    pl.ds(which * width + base * unit, together * unit),
                    :,
                ] = piece.astype(bf16)
    items = [extra[:, group * count : (group + 1) * count] for group in range(groups)]
    if ITEMS * groups < rows:
        items.append(jnp.zeros((rows - ITEMS * groups, count), f32))
    lines = jnp.concatenate(items, axis=0).T.reshape(blocks, unit, rows)
    out_ref[:, 3 * width :, :] = lines.astype(bf16)


def transform_kernel(groups, width, x_ref, own_ref, *refs):
    coarse, coarse_back, forward, backward = refs[0:2], refs[2:4], refs[4:6], refs[6:8]
    cos_ref, sin_ref, out_ref = refs[8:]
    blocks, lines, rows = x_ref.shape
    unit = width // groups
    count = blocks * unit
    together = 2 if groups % 2 == 0 else 1

    extra = x_ref[:, 3 * width :, :].astype(f32).reshape(count, rows)
    none = jnp.zeros((unit, rows), f32)
    before = jnp.concatenate([none, extra[: count - unit]], axis=0)
    after = jnp.concatenate([extra[unit:], none], axis=0)
    lane = lax.broadcasted_iota(jnp.int32, (count, rows), 1)
    item = lane % ITEMS

    def turn(value, steps):
        return value if steps % rows == 0 else pltpu.roll(value, steps % rows, 1)

    def own(tap):
        return jnp.broadcast_to(own_ref[tap][None], (blocks, unit, rows)).reshape(count, rows)

    middle = jnp.where(item % 2 == 0, turn(before, -9), turn(extra, 1))
    shorts = own(0) * extra + own(1) * middle + own(2) * turn(before, -8)
    edge_gated = shorts * turn(shorts, -2)
    edge_mixed = shorts * turn(extra, -2)

    def take(which, base):
        both = x_ref[:, pl.ds(which * width + base * unit, together * unit), :].astype(f32)
        signals = []
        for at in range(together):
            part = both[:, at * unit : (at + 1) * unit, :].reshape(count, rows)
            left = ITEMS * (base + at)
            scale = extra[:, left + 14 + which : left + 15 + which] * (1.0 / REACH)
            signal = decode(part) * scale
            if which == 0:
                signal = jnp.where(lane < 2, turn(edge_gated, -left), signal)
            if which == 2:
                signal = jnp.where(lane < 2, turn(edge_mixed, -left - 4), signal)
            signals.append(signal)
        return signals

    placed = jnp.zeros((count, rows), f32)
    for base in range(0, groups, together):
        cos, sin = cos_ref[...], sin_ref[...]
        taken = [take(which, base) for which in range(3)]
        stacked = jnp.concatenate(
            [taken[which][at] for at in range(together) for which in range(3)], axis=1
        )
        first = table_on_left(*coarse, stacked)
        lasts = []
        for at in range(together):
            spectra = []
            for which in range(3):
                here = slice((3 * at + which) * rows, (3 * at + which + 1) * rows)
                real, imag = first[:count, here], first[count:, here]
                turned = jnp.concatenate(
                    [real * cos + imag * sin, imag * cos - real * sin], axis=1
                )
                spectrum = table_on_right(turned, *forward)
                spectra.append((spectrum[:, :rows], spectrum[:, rows:]))
            (gr, gi), (hr, hi), (mr, mi) = spectra
            for real, imag in (
                (gr * hr - gi * hi, gr * hi + gi * hr),
                (mr * hr + mi * hi, mi * hr - mr * hi),
            ):
                product = jnp.concatenate([real, imag], axis=1)
                plain = table_on_right(product, *backward)
                real, imag = plain[:, :rows], plain[:, rows:]
                lasts.append(
                    jnp.concatenate([real * cos - imag * sin, imag * cos + real * sin], axis=0)
                )
        result = table_on_left(*coarse_back, jnp.concatenate(lasts, axis=1))
        for which in range(2):
            pieces = []
            for at in range(together):
                here = slice((2 * at + which) * rows, (2 * at + which + 1) * rows)
                part = result[:, here].reshape(blocks, unit, rows)
                scale = scale_of(
                    jnp.max(jnp.max(jnp.abs(part), axis=0), axis=1, keepdims=True)
                )
                words = encode(part, scale[None])
                pieces.append(words)
                left = ITEMS * (base + at) + 16 + 2 * which
                mine = turn(words.reshape(count, rows), left)
                placed = jnp.where((lane >= left) & (lane < left + 2), mine, placed)
                spot = ITEMS * (base + at) + 20 + which
                all_scale = jnp.broadcast_to(scale[None], (blocks, unit, rows))
                placed = jnp.where(lane == spot, all_scale.reshape(count, rows), placed)
            out_ref[:, pl.ds(which * width + base * unit, together * unit), :] = jnp.concatenate(
                pieces, axis=1
            ).astype(bf16)
    following = jnp.concatenate([placed[unit:], none], axis=0)
    placed = jnp.where(item < 20, following, placed)
    lines = jnp.where(item < 8, after, jnp.where(item < 14, before, placed))
    out_ref[:, 2 * width :, :] = lines.reshape(blocks, unit, rows).astype(bf16)


def finish_kernel(groups, y_ref, q_ref, k_ref, v_ref, g_ref, taps_ref, skip_ref, *refs):
    out_ref, gq_ref, gk_ref, gv_ref = refs
    rows, channels = q_ref.shape
    blocks = y_ref.shape[0]
    count = channels // groups
    unit = count // blocks
    width = unit * groups
    chunk = min(128, count)
    together = 2 if groups % 2 == 0 else 1
    extra = y_ref[:, 2 * width :, :].astype(f32).reshape(count, rows).T

    def one_chunk(group, inner, parts):
        start = group * count + inner
        lanes = pl.ds(start, chunk)
        skip = skip_ref[:, lanes]
        items = extra[ITEMS * group : ITEMS * (group + 1), inner : inner + chunk]
        after = [items[2 * at : 2 * at + 2] for at in range(4)]
        before = [items[8 + 2 * at : 10 + 2 * at] for at in range(3)]

        def arrived(which):
            scale = items[20 + which : 21 + which] * (1.0 / REACH)
            return (
                decode(parts[which]).T * scale,
                decode(items[16 + 2 * which : 18 + 2 * which]) * scale,
            )

        query, key = q_ref[:, lanes].astype(f32), k_ref[:, lanes].astype(f32)
        value, upstream = v_ref[:, lanes].astype(f32), g_ref[:, lanes].astype(f32)
        taps = [taps_at(taps_ref, which, lanes) for which in range(3)]
        shorts = [
            (
                short_forward(stream, taps[which], before[at]),
                short_after(stream, after[at], taps[which]),
            )
            for which, at, stream in ((0, 2, query), (1, 0, key), (2, 1, value))
        ]
        results = (arrived(0), arrived(1))
        upstreams = (upstream, after[3])
        grads = [[], [], []]
        for here in range(2):
            short_q, short_k, short_v = (short[here] for short in shorts)
            mixed = results[0][here] + skip * (short_k * short_v)
            if here == 0:
                out_ref[:, lanes] = (short_q * mixed).astype(bf16)
            grad_gated = results[1][here] + skip * (upstreams[here] * short_q)
            grads[0].append(upstreams[here] * mixed)
            grads[1].append(grad_gated * short_v)
            grads[2].append(grad_gated * short_k)
        for which, ref in enumerate((gq_ref, gk_ref, gv_ref)):
            rows_of, rim = grads[which]
            one, two, three = taps[which]
            ref[:, lanes] = (
                one * rows_of + two * ahead(rows_of, 1, rim) + three * ahead(rows_of, 2, rim)
            ).astype(bf16)

    for base in range(0, groups, together):
        for inner in range(0, count, chunk):
            both = [
                y_ref[
                    pl.ds(inner // unit, chunk // unit),
                    pl.ds(which * width + base * unit, together * unit),
                    :,
                ].astype(f32)
                for which in range(2)
            ]
            for at in range(together):
                parts = [
                    arrived[:, at * unit : (at + 1) * unit, :].reshape(chunk, rows)
                    for arrived in both
                ]
                one_chunk(base + at, inner, parts)


def local(query_in, key_in, value_in, conv_taps, long_filter, skip_gain, grad_out):
    rows, channels = query_in.shape
    blocks = lax.axis_size("inner") * lax.axis_size("outer")
    width = channels // blocks
    unit = 8 if width % 8 == 0 else width
    groups = width // unit
    large = pltpu.CompilerParams(vmem_limit_bytes=60 * 1024 * 1024)
    small = pltpu.CompilerParams(vmem_limit_bytes=24 * 1024 * 1024) if unit == 8 else large
    skip = skip_gain.reshape(1, channels)

    own = conv_taps.reshape(3, 3, groups, blocks, unit)
    own = lax.dynamic_index_in_dim(own, lax.axis_index(AXES), 3, keepdims=False)
    own = jnp.stack([own[1], own[2], own[0]])
    own = jnp.repeat(jnp.transpose(own, (1, 3, 2, 0)), 2, axis=3)
    own = jnp.pad(own, ((0, 0), (0, 0), (0, 0), (0, ITEMS - 6))).reshape(3, unit, ITEMS * groups)
    own = jnp.pad(own, ((0, 0), (0, 0), (0, rows - ITEMS * groups)))

    packed = pl.pallas_call(
        functools.partial(gate_kernel, groups),
        out_shape=jax.ShapeDtypeStruct((blocks, 3 * width + unit, rows), bf16),
        scratch_shapes=[pltpu.VMEM((ITEMS, channels), f32)],
        compiler_params=large,
        name="gate",
    )(query_in, key_in, value_in, grad_out, long_filter, conv_taps)
    spread = lax.all_to_all(packed, AXES, 0, 0, tiled=True)
    result = pl.pallas_call(
        functools.partial(transform_kernel, groups, width),
        out_shape=jax.ShapeDtypeStruct((blocks, 2 * width + unit, rows), bf16),
        compiler_params=small,
        name="transform",
    )(spread, own, *[jnp.asarray(table) for table in tables(blocks, rows, unit)])
    returned = lax.all_to_all(result, AXES, 0, 0, tiled=True)
    wide = jax.ShapeDtypeStruct((rows, channels), bf16)
    return pl.pallas_call(
        functools.partial(finish_kernel, groups),
        out_shape=(wide, wide, wide, wide),
        compiler_params=small,
        name="finish",
    )(returned, query_in, key_in, value_in, grad_out, conv_taps, skip)


def solution(mesh):
    split = P(AXES, None)
    return jax.shard_map(
        local,
        mesh=mesh,
        in_specs=(split, split, split, P(), split, P(), split),
        out_specs=(split, split, split, split),
        check_vma=False,
    )
```

time: 68.2 us -> 62.7 us (0.919)
  local copies, waits for them, and re-layouts: 12.3 us -> 0.74 us
  waiting for transfers between devices: 15.4 us -> 21.3 us
    unnamed x35 -> x33, local copies, waits for them, and re-layouts: 6.46 us -> 0.25 us
    all_to_all x1, waiting for transfers between devices: 15.4 us -> 21.3 us  [local(): spread = lax.all_to_all(packed, AXES, 0, 0, tiled=True)]
    pad x1, local copies, waits for them, and re-layouts: 1.43 us -> 0.01 us  [local(): jnp.pad(own, ((0, 0), (0, 0), (0, 0), (0, ITEMS - 6)))]
    pallas_call x1, Pallas kernels: 2.35 us -> 3.61 us  [local(): pl.pallas_call(functools.partial(gate_kernel, groups), out_shape=jax.Shap...]
    reshape x1, local copies, waits for them, and re-layouts: 1.2 us -> 0.34 us  [local(): own = conv_taps.reshape(3, 3, groups, blocks, unit)]
    slice x1, local copies, waits for them, and re-layouts: 0.86 us -> 0.03 us  [local(): own = jnp.stack([own[1], own[2], own[0]])]
    reshape x1 -> x0, local copies, waits for them, and re-layouts: 0.82 us -> none  [local(): taps = conv_taps.reshape(9, channels)]
    reshape x1, local copies, waits for them, and re-layouts: 0.89 us -> 0.09 us  [local(): jnp.pad(own, ((0, 0), (0, 0), (0, 0), (0, ITEMS - 6)))]
  transfers between devices with their start and end apart: 1 -> 1, of which waited for: 1 -> 1; matrix products, arithmetic and copies ran while one was open for 10% -> 1% of each run, Pallas kernels for 0% -> 0%
where the time goes in v2:
time: 62.7 us; the launch traced here: 62.4 us
  waiting for transfers between devices  21.3 us (34%)
  blocking collectives  20.2 us (32%)
  Pallas kernels  12.1 us (19%)
  starting transfers between devices  7.3 us (12%)
  between operations  0.89 us (1%)
  local copies, waits for them, and re-layouts  0.74 us (1%)
    all_to_all x1, waiting for transfers between devices, local(): spread = lax.all_to_all(packed, AXES, 0, 0, tiled=True)  21.3 us
    all_to_all x1, blocking collectives, local(): returned = lax.all_to_all(result, AXES, 0, 0, tiled=True)  20.2 us
    all_to_all x1, starting transfers between devices, local(): spread = lax.all_to_all(packed, AXES, 0, 0, tiled=True)  7.3 us
    pallas_call x1, Pallas kernels, local(): pl.pallas_call(functools.partial(transform_kernel, groups, width), out_sh...  5.68 us
    pallas_call x1, Pallas kernels, local(): pl.pallas_call(functools.partial(gate_kernel, groups), out_shape=jax.Shap...  3.61 us
    pallas_call x1, Pallas kernels, local(): pl.pallas_call(functools.partial(finish_kernel, groups), out_shape=(wide,...  2.79 us
  transfers between devices with their start and end apart: 1, of which 1 were waited for; matrix products, arithmetic and copies ran while one was open for 1% of the time, Pallas kernels for 0%

profile of v2, /device:TPU:0, one launch (start us, length us, event | category | flops | bytes accessed | tf_op | source)
XLA Modules:
  0.0 62.4 jit_solution(4962368633774453457)
XLA Ops:
  0.6 3.6 %gate.1 = bf16[32,104,128]{2,1,0:T(8,128)(2,1)} custom-call(bf16[128,1024]{1,0:T(8,128)(2,1)} %q_ref.3, bf16[128,1024]{1,0:T(8,128)(2,1)} %k_ref.3, bf16[128,1024]{1,0:T(8,128)(2,1)} %v_ref.3, bf16[128,1024]{1,0:T(8,128)(2,1)} %g_ref.3, f32[128,1024]{1,0:T(8,128)} %h_ref.1, f32[3,3,1024]{2,1,0:T(4,128)} %taps_ref.3), custom_call_target="tpu_custom_call" | custom-call | tf_op jit(solution)/shard_map/gate/pallas_call | solution.py:348
  4.2 0.0 copy-start.4
  4.2 0.0 copy-start.9
  4.2 0.0 copy-start.10
  4.3 0.0 copy-start.11
  4.3 0.0 copy-start.12
  4.3 0.0 copy-start.13
  4.3 0.0 copy-start.14
  4.3 7.3 %all-to-all-start = ((bf16[32,104,128]{2,1,0:T(8,128)(2,1)}), bf16[32,104,128]{2,1,0:T(8,128)(2,1)S(1)}, u32[]{:S(2)}, u32[]{:S(2)}) async-start(bf16[32,104,128]{2,1,0:T(8,128)(2,1)} %gate.1), calls=%async_computation | async-start | bytes 1703936 | tf_op jit(solution)/shard_map/all_to_all | solution.py:355
  11.6 0.0 copy-done.4
  11.6 0.0 copy-start.6
  11.6 0.0 copy-start.7
  11.6 0.0 copy-start.8
  11.7 0.3 reshape.23
  12.0 0.0 copy-start.5
  12.1 0.2 copy.25
  12.3 0.1 reshape.25.own_ref
  12.4 21.3 %all-to-all-done.x_ref = bf16[32,104,128]{2,1,0:T(8,128)(2,1)S(1)} async-done(((bf16[32,104,128]{2,1,0:T(8,128)(2,1)}), bf16[32,104,128]{2,1,0:T(8,128)(2,1)S(1)}, u32[]{:S(2)}, u32[]{:S(2)}) %all-to-all-start) | async-done | bytes 852000 | tf_op jit(solution)/shard_map/all_to_all | solution.py:355
  33.6 0.0 copy-done.9
  33.6 0.0 copy-done.10
  33.6 0.0 copy-done.11
  33.6 0.0 copy-done.12
  33.7 0.0 copy-done.13
  33.7 0.0 copy-done.14
  33.7 0.0 copy-done.6
  33.7 0.0 copy-done.7
  33.7 0.0 copy-done.8
  33.7 0.0 copy-done.5
  33.7 5.7 %transform.1 = bf16[32,72,128]{2,1,0:T(8,128)(2,1)S(1)} custom-call(bf16[32,104,128]{2,1,0:T(8,128)(2,1)S(1)} %all-to-all-done.x_ref, f32[3,8,128]{2,1,0:T(8,128)S(1)} %reshape.25.own_ref, bf16[512,256]{1,0:T(8,128)(2,1)S(1)} %copy-done.5, bf16[512,256]{1,0:T(8,128)(2,1)S(1)} %copy-done.6, bf16[256,512]{1,0:T(8,128)(2,1)S(1)} %copy-done.7, ...), custom_call_target="tpu_custom_call" | custom-call | tf_op jit(solution)/shard_map/transform/pallas_call | solution.py:356
  39.4 0.0 copy-start
  39.4 0.0 copy-start.1
  39.4 0.0 copy-start.2
  39.4 0.0 copy-start.3
  39.5 0.0 copy-start.15
  39.5 20.2 %all_to_all.10.y_ref = bf16[32,72,128]{2,1,0:T(8,128)(2,1)S(1)} all-to-all(bf16[32,72,128]{2,1,0:T(8,128)(2,1)S(1)} %transform.1), channel_id=1, replica_groups=mesh['outer'=8,'inner'=4] {'outer','inner'}, dimensions={0} | all-to-all | bytes 1179648 | tf_op jit(solution)/shard_map/all_to_all | solution.py:362
  59.6 0.0 copy-done
  59.6 0.0 copy-done.1
  59.6 0.0 copy-done.2
  59.6 0.0 copy-done.3
  59.7 0.0 copy-done.15
  59.7 2.8 %finish.1 = (bf16[128,1024]{1,0:T(8,128)(2,1)}, bf16[128,1024]{1,0:T(8,128)(2,1)}, bf16[128,1024]{1,0:T(8,128)(2,1)}, bf16[128,1024]{1,0:T(8,128)(2,1)}) custom-call(bf16[32,72,128]{2,1,0:T(8,128)(2,1)S(1)} %all_to_all.10.y_ref, bf16[128,1024]{1,0:T(8,128)(2,1)S(1)} %copy-done, bf16[128,1024]{1,0:T(8,128)(2,1)S(1)} %copy-done.1, ...), custom_call_target="tpu_custom_call" | custom-call | tf_op jit(solution)/shard_map/finish/pallas_call | solution.py:364
  (5 shorter events, 0.1 us)
Async XLA Ops:
  4.2 7.4 %copy-start.4 = (f32[3,3,1024]{2,1,0:T(4,128)S(1)}, f32[3,3,1024]{2,1,0:T(4,128)}, u32[]{:S(2)}) copy-start(f32[3,3,1024]{2,1,0:T(4,128)} %taps_ref.3) | copy-start | bytes 110596
  4.2 29.4 %copy-start.9 = (bf16[256,256]{1,0:T(8,128)(2,1)S(1)}, bf16[256,256]{1,0:T(8,128)(2,1)}, u32[]{:S(2)}) copy-start(bf16[256,256]{1,0:T(8,128)(2,1)} %constant.44.clone.refs_4_) | copy-start | bytes 393220
  4.2 29.4 %copy-start.10 = (bf16[256,256]{1,0:T(8,128)(2,1)S(1)}, bf16[256,256]{1,0:T(8,128)(2,1)}, u32[]{:S(2)}) copy-start(bf16[256,256]{1,0:T(8,128)(2,1)} %constant.45.clone.refs_5_) | copy-start | bytes 393220
  4.3 29.4 %copy-start.11 = (bf16[256,256]{1,0:T(8,128)(2,1)S(1)}, bf16[256,256]{1,0:T(8,128)(2,1)}, u32[]{:S(2)}) copy-start(bf16[256,256]{1,0:T(8,128)(2,1)} %constant.46.clone.refs_6_) | copy-start | bytes 393220
  4.3 29.4 %copy-start.12 = (bf16[256,256]{1,0:T(8,128)(2,1)S(1)}, bf16[256,256]{1,0:T(8,128)(2,1)}, u32[]{:S(2)}) copy-start(bf16[256,256]{1,0:T(8,128)(2,1)} %constant.47.clone.refs_7_) | copy-start | bytes 393220
  4.3 29.4 %copy-start.13 = (f32[256,128]{1,0:T(8,128)S(1)}, f32[256,128]{1,0:T(8,128)}, u32[]{:S(2)}) copy-start(f32[256,128]{1,0:T(8,128)} %constant.48.clone.refs_8_) | copy-start | bytes 393220
  4.3 29.4 %copy-start.14 = (f32[256,128]{1,0:T(8,128)S(1)}, f32[256,128]{1,0:T(8,128)}, u32[]{:S(2)}) copy-start(f32[256,128]{1,0:T(8,128)} %constant.49.clone.refs_9_) | copy-start | bytes 393220
  4.3 29.3 %all-to-all-start = ((bf16[32,104,128]{2,1,0:T(8,128)(2,1)}), bf16[32,104,128]{2,1,0:T(8,128)(2,1)S(1)}, u32[]{:S(2)}, u32[]{:S(2)}) async-start(bf16[32,104,128]{2,1,0:T(8,128)(2,1)} %gate.1), calls=%async_computation | async-start | bytes 1703936 | tf_op jit(solution)/shard_map/all_to_all | solution.py:355
  11.6 22.1 %copy-start.6 = (bf16[512,256]{1,0:T(8,128)(2,1)S(1)}, bf16[512,256]{1,0:T(8,128)(2,1)}, u32[]{:S(2)}) copy-start(bf16[512,256]{1,0:T(8,128)(2,1)} %constant.41.clone.refs_1_) | copy-start | bytes 786436
  11.6 22.1 %copy-start.7 = (bf16[256,512]{1,0:T(8,128)(2,1)S(1)}, bf16[256,512]{1,0:T(8,128)(2,1)}, u32[]{:S(2)}) copy-start(bf16[256,512]{1,0:T(8,128)(2,1)} %constant.42.clone.refs_2_) | copy-start | bytes 786436
  11.6 22.1 %copy-start.8 = (bf16[256,512]{1,0:T(8,128)(2,1)S(1)}, bf16[256,512]{1,0:T(8,128)(2,1)}, u32[]{:S(2)}) copy-start(bf16[256,512]{1,0:T(8,128)(2,1)} %constant.43.clone.refs_3_) | copy-start | bytes 786436
  12.0 21.7 %copy-start.5 = (bf16[512,256]{1,0:T(8,128)(2,1)S(1)}, bf16[512,256]{1,0:T(8,128)(2,1)}, u32[]{:S(2)}) copy-start(bf16[512,256]{1,0:T(8,128)(2,1)} %constant.40.clone.refs_0_) | copy-start | bytes 786436
  39.4 20.2 %copy-start = (bf16[128,1024]{1,0:T(8,128)(2,1)S(1)}, bf16[128,1024]{1,0:T(8,128)(2,1)}, u32[]{:S(2)}) copy-start(bf16[128,1024]{1,0:T(8,128)(2,1)} %q_ref.3) | copy-start | bytes 786436
  39.4 20.2 %copy-start.1 = (bf16[128,1024]{1,0:T(8,128)(2,1)S(1)}, bf16[128,1024]{1,0:T(8,128)(2,1)}, u32[]{:S(2)}) copy-start(bf16[128,1024]{1,0:T(8,128)(2,1)} %k_ref.3) | copy-start | bytes 786436
  39.4 20.2 %copy-start.2 = (bf16[128,1024]{1,0:T(8,128)(2,1)S(1)}, bf16[128,1024]{1,0:T(8,128)(2,1)}, u32[]{:S(2)}) copy-start(bf16[128,1024]{1,0:T(8,128)(2,1)} %v_ref.3) | copy-start | bytes 786436
  39.4 20.2 %copy-start.3 = (bf16[128,1024]{1,0:T(8,128)(2,1)S(1)}, bf16[128,1024]{1,0:T(8,128)(2,1)}, u32[]{:S(2)}) copy-start(bf16[128,1024]{1,0:T(8,128)(2,1)} %g_ref.3) | copy-start | bytes 786436
  39.5 20.2 %copy-start.15 = (f32[1024]{0:T(1024)S(1)}, f32[1024]{0:T(1024)}, u32[]{:S(2)}) copy-start(f32[1024]{0:T(1024)} %param.22) | copy-start | bytes 12292

commit v3 on v2

--- a/solution.py
+++ b/solution.py
@@ -46,15 +46,15 @@
     return high, low
 
 
-def table_on_left(high_ref, low_ref, value):
+def table_on_left(high_table, low_table, value):
     high, low = split_pair(value)
-    table = jnp.concatenate([high_ref[...], high_ref[...], low_ref[...]], axis=1)
+    table = jnp.concatenate([high_table, high_table, low_table], axis=1)
     return jnp.dot(table, jnp.concatenate([high, low, high], axis=0), preferred_element_type=f32)
 
 
-def table_on_right(value, high_ref, low_ref):
+def table_on_right(value, high_table, low_table):
     high, low = split_pair(value)
-    table = jnp.concatenate([high_ref[...], low_ref[...], high_ref[...]], axis=0)
+    table = jnp.concatenate([high_table, low_table, high_table], axis=0)
     return jnp.dot(jnp.concatenate([high, high, low], axis=1), table, preferred_element_type=f32)
 
 
@@ -73,18 +73,39 @@
     cos, sin = np.cos(fine), np.sin(fine)
     forward = np.block([[cos, -sin], [sin, cos]])
     backward = np.block([[cos, sin], [-sin, cos]])
-    flat = [half for table in (coarse, coarse_back, forward, backward) for half in numpy_pair(table)]
-    return flat + [np.cos(twist).astype(np.float32), np.sin(twist).astype(np.float32)]
+    columns = 2 * rows
+    twists = np.concatenate([np.cos(twist), np.sin(twist)], axis=1)
+    flat = []
+    for table in (coarse, coarse_back, forward, backward, twists):
+        for half in numpy_pair(table):
+            flat += np.split(half, table.shape[1] // columns, axis=1)
+    return np.concatenate(flat)
+
+
+def unpack_tables(ref, count, rows):
+    columns = 2 * rows
+    shapes = [(2 * count, count)] * 2 + [(count, 2 * count)] * 2 + [(columns, columns)] * 4
+    shapes += [(count, columns)] * 2
+    found, at = [], 0
+    for height, length in shapes:
+        parts = []
+        for _ in range(length // columns):
+            parts.append(ref[at : at + height])
+            at += height
+        found.append(jnp.concatenate(parts, axis=1) if len(parts) > 1 else parts[0])
+    twists = found[8].astype(f32) + found[9].astype(f32)
+    return found[0:2], found[2:4], found[4:6], found[6:8], twists[:, :rows], twists[:, rows:]
 
 
 def shifted(stream, steps, rim):
     rolled = pltpu.roll(stream, steps, 0)
     if rim is None:
         return rolled
-    row = lax.broadcasted_iota(jnp.int32, stream.shape, 0)
-    if steps == 1:
-        return jnp.where(row == 0, rim[1:2], rolled)
-    return jnp.where(row == 0, rim[0:1], jnp.where(row == 1, rim[1:2], rolled))
+    edge = rolled[:8]
+    row = lax.broadcasted_iota(jnp.int32, edge.shape, 0)
+    for at in range(steps):
+        edge = jnp.where(row == at, rim[2 - steps + at : 3 - steps + at], edge)
+    return jnp.concatenate([edge, rolled[8:]], axis=0)
 
 
 def short_forward(stream, taps, rim):
@@ -103,67 +124,119 @@
 def ahead(rows, steps, rim):
     count = rows.shape[0]
     rolled = pltpu.roll(rows, count - steps, 0)
-    row = lax.broadcasted_iota(jnp.int32, rows.shape, 0)
-    if steps == 1:
-        return jnp.where(row == count - 1, rim[0:1], rolled)
-    return jnp.where(row == count - 2, rim[0:1], jnp.where(row == count - 1, rim[1:2], rolled))
-
-
-def gate_kernel(groups, q_ref, k_ref, v_ref, g_ref, h_ref, taps_ref, out_ref, extra):
+    edge = rolled[count - 8 :]
+    row = lax.broadcasted_iota(jnp.int32, edge.shape, 0)
+    for at in range(steps):
+        edge = jnp.where(row == 8 - steps + at, rim[at : at + 1], edge)
+    return jnp.concatenate([rolled[: count - 8], edge], axis=0)
+
+
+def slices_of(channels):
+    size = min(256, channels)
+    return [pl.ds(start, size) for start in range(0, channels, size)]
+
+
+def gate_kernel(unit, q_hbm, k_hbm, v_hbm, g_hbm, h_hbm, taps_hbm, out_hbm, *scratch):
+    q_ref, k_ref, v_ref, g_ref, h_ref, taps_ref, out_ref, extra, sems, out_sems = scratch
     rows, channels = q_ref.shape
     blocks = out_ref.shape[0]
-    count = channels // groups
-    unit = count // blocks
-    width = unit * groups
-    chunk = min(128, count)
-    together = 2 if groups % 2 == 0 else 1
+    width = channels // blocks
+    run = min(width, 2 * unit)
+    span = run * blocks
+    chunk = 128
+    starts = range(0, channels, chunk)
+    pairs = (
+        (taps_hbm, taps_ref),
+        (k_hbm, k_ref),
+        (v_hbm, v_ref),
+        (q_hbm, q_ref),
+        (g_hbm, g_ref),
+        (h_hbm, h_ref),
+    )
+    copies = [
+        pltpu.make_async_copy(hbm, ref, sems.at[at]) for at, (hbm, ref) in enumerate(pairs)
+    ]
+    for copy in copies:
+        copy.start()
     extra[14:ITEMS, :] = jnp.zeros((ITEMS - 14, channels), f32)
-
-    def words(start):
+    row = lax.broadcasted_iota(jnp.int32, (8, chunk), 0)
+
+    def short(ref, tap_row, item, lanes):
+        stream = ref[:, lanes].astype(f32)
+        extra[2 * item : 2 * item + 2, lanes] = stream[0:2]
+        extra[8 + 2 * item : 10 + 2 * item, lanes] = stream[rows - 2 :]
+        return short_forward(stream, taps_at(taps_ref, tap_row, lanes), None)
+
+    def send(which, start, signal):
         lanes = pl.ds(start, chunk)
-        query, key = q_ref[:, lanes].astype(f32), k_ref[:, lanes].astype(f32)
-        value, upstream = v_ref[:, lanes].astype(f32), g_ref[:, lanes].astype(f32)
-        for at, stream in enumerate((key, value, query, upstream)):
-            extra[2 * at : 2 * at + 2, lanes] = stream[0:2]
-        for at, stream in enumerate((key, value, query)):
-            extra[8 + 2 * at : 10 + 2 * at, lanes] = stream[rows - 2 :]
-        short_q = short_forward(query, taps_at(taps_ref, 0, lanes), None)
-        short_k = short_forward(key, taps_at(taps_ref, 1, lanes), None)
-        short_v = short_forward(value, taps_at(taps_ref, 2, lanes), None)
-        result = []
-        row = lax.broadcasted_iota(jnp.int32, (8, chunk), 0)
-        for which, signal in enumerate((short_k * short_v, h_ref[:, lanes], upstream * short_q)):
-            if which != 1:
-                edge = jnp.where(row < 2, 0.0, signal[:8])
-                signal = jnp.concatenate([edge, signal[8:]], axis=0)
-            scale = scale_of(jnp.max(jnp.abs(signal), axis=0, keepdims=True))
-            extra[14 + which : 15 + which, lanes] = scale
-            result.append(encode(signal, scale).T.reshape(chunk // unit, unit, rows))
-        return result
-
-    for base in range(0, groups, together):
-        for inner in range(0, count, chunk):
-            pieces = [words((base + at) * count + inner) for at in range(together)]
-            for which in range(3):
-                piece = jnp.concatenate([part[which] for part in pieces], axis=1)
-                out_ref[
-                    pl.ds(inner // unit, chunk // unit),
-                    pl.ds(which * width + base * unit, together * unit),
-                    :,
-                ] = piece.astype(bf16)
-    items = [extra[:, group * count : (group + 1) * count] for group in range(groups)]
-    if ITEMS * groups < rows:
-        items.append(jnp.zeros((rows - ITEMS * groups, count), f32))
-    lines = jnp.concatenate(items, axis=0).T.reshape(blocks, unit, rows)
-    out_ref[:, 3 * width :, :] = lines.astype(bf16)
-
-
-def transform_kernel(groups, width, x_ref, own_ref, *refs):
-    coarse, coarse_back, forward, backward = refs[0:2], refs[2:4], refs[4:6], refs[6:8]
-    cos_ref, sin_ref, out_ref = refs[8:]
+        first, line = start % span // run, start // span * run
+        if which != 1:
+            edge = jnp.where(row < 2, 0.0, signal[:8])
+            signal = jnp.concatenate([edge, signal[8:]], axis=0)
+        scale = scale_of(jnp.max(jnp.abs(signal), axis=0, keepdims=True))
+        extra[14 + which : 15 + which, lanes] = scale
+        words = encode(signal, scale)
+        if run % 16 == 0:
+            words = words.astype(bf16).T.reshape(chunk // run, run, rows)
+        else:
+            words = words.T.reshape(chunk // run, run, rows).astype(bf16)
+        out_ref[pl.ds(first, chunk // run), pl.ds(which * width + line, run), :] = words
+
+    outs = []
+
+    def leave(at, first, count):
+        if run % 16 == 0:
+            part = (slice(None), pl.ds(first, count))
+            copy = pltpu.make_async_copy(out_ref.at[part], out_hbm.at[part], out_sems.at[at])
+            copy.start()
+            outs.append(copy)
+
+    for copy in copies[:3]:
+        copy.wait()
+    for start in starts:
+        lanes = pl.ds(start, chunk)
+        send(0, start, short(k_ref, 1, 0, lanes) * short(v_ref, 2, 1, lanes))
+    leave(0, 0, width)
+    copies[3].wait()
+    copies[4].wait()
+    for start in starts:
+        lanes = pl.ds(start, chunk)
+        upstream = g_ref[:, lanes].astype(f32)
+        extra[6:8, lanes] = upstream[0:2]
+        send(2, start, upstream * short(q_ref, 0, 2, lanes))
+    leave(2, 2 * width, width)
+    copies[5].wait()
+    for start in starts:
+        send(1, start, h_ref[:, pl.ds(start, chunk)])
+    leave(1, width, width)
+    halves = run // unit
+    items = []
+    for start in range(0, channels, span):
+        items += [extra[:, start : start + span]] * halves
+    if ITEMS * len(items) < rows:
+        items.append(jnp.zeros((rows - ITEMS * len(items), span), f32))
+    lines = jnp.concatenate(items, axis=0).T.reshape(blocks, run, rows)
+    lane = lax.broadcasted_iota(jnp.int32, (blocks, unit, rows), 2)
+    merged = lines[:, :unit, :]
+    for half in range(1, halves):
+        part = lines[:, half * unit : (half + 1) * unit, :]
+        merged = jnp.where(lane // ITEMS % halves == half, part, merged)
+    out_ref[:, 3 * width :, :] = merged.astype(bf16)
+    if run % 16 == 0:
+        leave(3, 3 * width, unit)
+    else:
+        copy = pltpu.make_async_copy(out_ref, out_hbm, out_sems.at[0])
+        copy.start()
+        outs.append(copy)
+    for copy in outs:
+        copy.wait()
+
+
+def transform_kernel(groups, width, x_ref, own_ref, table_ref, out_ref):
     blocks, lines, rows = x_ref.shape
     unit = width // groups
     count = blocks * unit
+    coarse, coarse_back, forward, backward, cos, sin = unpack_tables(table_ref, count, rows)
     together = 2 if groups % 2 == 0 else 1
 
     extra = x_ref[:, 3 * width :, :].astype(f32).reshape(count, rows)
@@ -201,7 +274,6 @@
 
     placed = jnp.zeros((count, rows), f32)
     for base in range(0, groups, together):
-        cos, sin = cos_ref[...], sin_ref[...]
         taken = [take(which, base) for which in range(3)]
         stacked = jnp.concatenate(
             [taken[which][at] for at in range(together) for which in range(3)], axis=1
@@ -255,42 +327,76 @@
     out_ref[:, 2 * width :, :] = lines.reshape(blocks, unit, rows).astype(bf16)
 
 
-def finish_kernel(groups, y_ref, q_ref, k_ref, v_ref, g_ref, taps_ref, skip_ref, *refs):
-    out_ref, gq_ref, gk_ref, gv_ref = refs
+def prepare_kernel(q_ref, k_ref, v_ref, taps_ref, short_ref, tail_ref, ready_ref):
     rows, channels = q_ref.shape
+    chunk = 128
+    none = jnp.zeros((2, chunk), f32)
+    ready_ref[...] = jnp.ones(ready_ref.shape, f32)
+    for start in range(0, channels, chunk):
+        lanes = pl.ds(start, chunk)
+        for which, ref in enumerate((q_ref, k_ref, v_ref)):
+            stream = ref[:, lanes].astype(f32)
+            tail_ref[which, :, lanes] = stream[rows - 8 :]
+            short_ref[which, :, lanes] = short_forward(
+                stream, taps_at(taps_ref, which, lanes), none
+            )
+
+
+def finish_kernel(
+    unit, y_ref, g_ref, short_ref, tail_ref, taps_ref, skip_ref, *refs
+):
+    targets, held, sems = refs[:4], refs[4:8], refs[8]
+    rows, channels = g_ref.shape
     blocks = y_ref.shape[0]
-    count = channels // groups
-    unit = count // blocks
-    width = unit * groups
-    chunk = min(128, count)
-    together = 2 if groups % 2 == 0 else 1
-    extra = y_ref[:, 2 * width :, :].astype(f32).reshape(count, rows).T
-
-    def one_chunk(group, inner, parts):
-        start = group * count + inner
+    width = channels // blocks
+    run = min(width, 2 * unit)
+    span = run * blocks
+    chunk = 128
+    halves = run // unit
+    slices = slices_of(channels)
+    copies = []
+    extra = y_ref[:, 2 * width :, :].astype(f32).reshape(blocks * unit, rows)
+    parts = [extra] + [pltpu.roll(extra, rows - half * ITEMS, 1) for half in range(1, halves)]
+    parts = [part.reshape(blocks, unit, rows) for part in parts]
+    extra = jnp.concatenate(parts, axis=1).reshape(span, rows).T
+    row = lax.broadcasted_iota(jnp.int32, (8, chunk), 0)
+    for start in range(0, channels, chunk):
         lanes = pl.ds(start, chunk)
+        first, line = start % span // run, start // span * run
         skip = skip_ref[:, lanes]
-        items = extra[ITEMS * group : ITEMS * (group + 1), inner : inner + chunk]
+        top, inner = start // span * halves * ITEMS, start % span
+        items = extra[top : top + ITEMS, inner : inner + chunk]
         after = [items[2 * at : 2 * at + 2] for at in range(4)]
         before = [items[8 + 2 * at : 10 + 2 * at] for at in range(3)]
 
         def arrived(which):
+            part = y_ref[pl.ds(first, chunk // run), pl.ds(which * width + line, run), :]
+            if run % 16 == 0:
+                part = part.reshape(chunk, rows).T.astype(f32)
+            else:
+                part = part.astype(f32).reshape(chunk, rows).T
             scale = items[20 + which : 21 + which] * (1.0 / REACH)
-            return (
-                decode(parts[which]).T * scale,
-                decode(items[16 + 2 * which : 18 + 2 * which]) * scale,
+            return decode(part) * scale, decode(items[16 + 2 * which : 18 + 2 * which]) * scale
+
+        upstream = g_ref[:, lanes].astype(f32)
+        taps = [taps_at(taps_ref, which, lanes) for which in range(3)]
+        shorts = []
+        for which, at in ((0, 2), (1, 0), (2, 1)):
+            one, two, three = taps[which]
+            past = before[at]
+            short = short_ref[which, :, lanes]
+            edge = short[:8] + jnp.where(
+                row == 0,
+                two * past[1:2] + three * past[0:1],
+                jnp.where(row == 1, three * past[1:2], 0.0),
             )
-
-        query, key = q_ref[:, lanes].astype(f32), k_ref[:, lanes].astype(f32)
-        value, upstream = v_ref[:, lanes].astype(f32), g_ref[:, lanes].astype(f32)
-        taps = [taps_at(taps_ref, which, lanes) for which in range(3)]
-        shorts = [
-            (
-                short_forward(stream, taps[which], before[at]),
-                short_after(stream, after[at], taps[which]),
+            tail = tail_ref[which, :, lanes]
+            shorts.append(
+                (
+                    jnp.concatenate([edge, short[8:]], axis=0),
+                    short_after(tail, after[at], taps[which]),
+                )
             )
-            for which, at, stream in ((0, 2, query), (1, 0, key), (2, 1, value))
-        ]
         results = (arrived(0), arrived(1))
         upstreams = (upstream, after[3])
         grads = [[], [], []]
@@ -298,34 +404,28 @@
             short_q, short_k, short_v = (short[here] for short in shorts)
             mixed = results[0][here] + skip * (short_k * short_v)
             if here == 0:
-                out_ref[:, lanes] = (short_q * mixed).astype(bf16)
+                held[0][:, lanes] = (short_q * mixed).astype(bf16)
             grad_gated = results[1][here] + skip * (upstreams[here] * short_q)
             grads[0].append(upstreams[here] * mixed)
             grads[1].append(grad_gated * short_v)
             grads[2].append(grad_gated * short_k)
-        for which, ref in enumerate((gq_ref, gk_ref, gv_ref)):
+        for which in range(3):
             rows_of, rim = grads[which]
             one, two, three = taps[which]
-            ref[:, lanes] = (
+            held[1 + which][:, lanes] = (
                 one * rows_of + two * ahead(rows_of, 1, rim) + three * ahead(rows_of, 2, rim)
             ).astype(bf16)
-
-    for base in range(0, groups, together):
-        for inner in range(0, count, chunk):
-            both = [
-                y_ref[
-                    pl.ds(inner // unit, chunk // unit),
-                    pl.ds(which * width + base * unit, together * unit),
-                    :,
-                ].astype(f32)
-                for which in range(2)
-            ]
-            for at in range(together):
-                parts = [
-                    arrived[:, at * unit : (at + 1) * unit, :].reshape(chunk, rows)
-                    for arrived in both
-                ]
-                one_chunk(base + at, inner, parts)
+        if (start + chunk) % slices[0].size == 0:
+            at = start // slices[0].size
+            for which in range(4):
+                part = (slice(None), slices[at])
+                copy = pltpu.make_async_copy(
+                    held[which].at[part], targets[which].at[part], sems.at[at, which]
+                )
+                copy.start()
+                copies.append(copy)
+    for copy in copies:
+        copy.wait()
 
 
 def local(query_in, key_in, value_in, conv_taps, long_filter, skip_gain, grad_out):
@@ -338,35 +438,68 @@
     small = pltpu.CompilerParams(vmem_limit_bytes=24 * 1024 * 1024) if unit == 8 else large
     skip = skip_gain.reshape(1, channels)
 
-    own = conv_taps.reshape(3, 3, groups, blocks, unit)
+    run = min(width, 2 * unit)
+    own = conv_taps.reshape(3, 3, width // run, blocks, run)
     own = lax.dynamic_index_in_dim(own, lax.axis_index(AXES), 3, keepdims=False)
+    own = own.reshape(3, 3, groups, unit)
     own = jnp.stack([own[1], own[2], own[0]])
     own = jnp.repeat(jnp.transpose(own, (1, 3, 2, 0)), 2, axis=3)
     own = jnp.pad(own, ((0, 0), (0, 0), (0, 0), (0, ITEMS - 6))).reshape(3, unit, ITEMS * groups)
     own = jnp.pad(own, ((0, 0), (0, 0), (0, rows - ITEMS * groups)))
 
+    far = pl.BlockSpec(memory_space=pltpu.HBM)
+    near = pl.BlockSpec(memory_space=pltpu.VMEM)
+    stream = pltpu.VMEM((rows, channels), bf16)
+    parts = len(slices_of(channels))
     packed = pl.pallas_call(
-        functools.partial(gate_kernel, groups),
+        functools.partial(gate_kernel, unit),
         out_shape=jax.ShapeDtypeStruct((blocks, 3 * width + unit, rows), bf16),
-        scratch_shapes=[pltpu.VMEM((ITEMS, channels), f32)],
+        in_specs=[far] * 6,
+        out_specs=far,
+        scratch_shapes=[
+            *[stream] * 4,
+            pltpu.VMEM((rows, channels), f32),
+            pltpu.VMEM((3, 3, channels), f32),
+            pltpu.VMEM((blocks, 3 * width + unit, rows), bf16),
+            pltpu.VMEM((ITEMS, channels), f32),
+            pltpu.SemaphoreType.DMA((6,)),
+            pltpu.SemaphoreType.DMA((4,)),
+        ],
         compiler_params=large,
         name="gate",
     )(query_in, key_in, value_in, grad_out, long_filter, conv_taps)
     spread = lax.all_to_all(packed, AXES, 0, 0, tiled=True)
+    short, tail, ready = pl.pallas_call(
+        prepare_kernel,
+        out_shape=(
+            jax.ShapeDtypeStruct((3, rows, channels), f32),
+            jax.ShapeDtypeStruct((3, 8, channels), f32),
+            jax.ShapeDtypeStruct((unit, rows), f32),
+        ),
+        compiler_params=large,
+        cost_estimate=pl.CostEstimate(
+            flops=30 * rows * channels, bytes_accessed=20 * rows * channels, transcendentals=0
+        ),
+        name="prepare",
+    )(query_in, key_in, value_in, conv_taps)
     result = pl.pallas_call(
         functools.partial(transform_kernel, groups, width),
         out_shape=jax.ShapeDtypeStruct((blocks, 2 * width + unit, rows), bf16),
+        in_specs=[near, near, near],
         compiler_params=small,
         name="transform",
-    )(spread, own, *[jnp.asarray(table) for table in tables(blocks, rows, unit)])
+    )(spread, own * ready, jnp.asarray(tables(blocks, rows, unit)))
     returned = lax.all_to_all(result, AXES, 0, 0, tiled=True)
     wide = jax.ShapeDtypeStruct((rows, channels), bf16)
     return pl.pallas_call(
-        functools.partial(finish_kernel, groups),
+        functools.partial(finish_kernel, unit),
         out_shape=(wide, wide, wide, wide),
+        in_specs=[near] * 6,
+        out_specs=(far, far, far, far),
+        scratch_shapes=[*[stream] * 4, pltpu.SemaphoreType.DMA((parts, 4))],
         compiler_params=small,
         name="finish",
-    )(returned, query_in, key_in, value_in, grad_out, conv_taps, skip)
+    )(returned, grad_out, short, tail, conv_taps, skip)
 
 
 def solution(mesh):

time: 62.7 us -> 61.6 us (0.982)
  waiting for transfers between devices: 21.3 us -> 17.7 us
  Pallas kernels: 12.1 us -> 13.9 us
  other arithmetic: 0.01 us -> 0.7 us
    all_to_all x1, waiting for transfers between devices: 21.3 us -> 17.7 us  [local(): spread = lax.all_to_all(packed, AXES, 0, 0, tiled=True)]
    pallas_call x2 -> x3, Pallas kernels: 6.4 us -> 8.26 us  [the longest x1 3.3 us: local(): pl.pallas_call(functools.partial(gate_kernel, unit), out_shape=jax.ShapeD...]
    mul x0 -> x1, other arithmetic: none -> 0.69 us  [local(): own * ready]
  transfers between devices with their start and end apart: 1 -> 1, of which waited for: 1 -> 1; matrix products, arithmetic and copies ran while one was open for 1% -> 2% of each run, Pallas kernels for 0% -> 5%
where the time goes in v3:
time: 61.6 us; the launch traced here: 61.3 us
  blocking collectives  20.2 us (33%)
  waiting for transfers between devices  17.7 us (29%)
  Pallas kernels  13.9 us (23%)
  starting transfers between devices  7.3 us (12%)
  local copies, waits for them, and re-layouts  0.75 us (1%)
  between operations  0.75 us (1%)
  other arithmetic  0.7 us (1%)
    all_to_all x1, blocking collectives, local(): returned = lax.all_to_all(result, AXES, 0, 0, tiled=True)  20.2 us
    all_to_all x1, waiting for transfers between devices, local(): spread = lax.all_to_all(packed, AXES, 0, 0, tiled=True)  17.7 us
    all_to_all x1, starting transfers between devices, local(): spread = lax.all_to_all(packed, AXES, 0, 0, tiled=True)  7.3 us
    pallas_call x1, Pallas kernels, local(): pl.pallas_call(functools.partial(transform_kernel, groups, width), out_sh...  5.69 us
    pallas_call x1, Pallas kernels, local(): pl.pallas_call(functools.partial(gate_kernel, unit), out_shape=jax.ShapeD...  3.3 us
    pallas_call x1, Pallas kernels, local(): pl.pallas_call(prepare_kernel, out_shape=(jax.ShapeDtypeStruct((3, rows,...  2.81 us
    pallas_call x1, Pallas kernels, local(): pl.pallas_call(functools.partial(finish_kernel, unit), out_shape=(wide, w...  2.15 us
  transfers between devices with their start and end apart: 1, of which 1 were waited for; matrix products, arithmetic and copies ran while one was open for 2% of the time, Pallas kernels for 5%

profile of v3, /device:TPU:0, one launch (start us, length us, event | category | flops | bytes accessed | tf_op | source)
XLA Modules:
  0.0 61.3 jit_solution(12297667681072694770)
XLA Ops:
  0.6 0.0 copy-start.3
  0.6 3.3 %gate.1 = bf16[32,104,128]{2,1,0:T(8,128)(2,1)} custom-call(bf16[128,1024]{1,0:T(8,128)(2,1)} %q_ref.1, bf16[128,1024]{1,0:T(8,128)(2,1)} %k_ref.1, bf16[128,1024]{1,0:T(8,128)(2,1)} %v_ref.1, bf16[128,1024]{1,0:T(8,128)(2,1)} %g_ref.1, f32[128,1024]{1,0:T(8,128)} %h_hbm.1, f32[3,3,1024]{2,1,0:T(4,128)} %taps_ref.3), custom_call_target="tpu_custom_call" | custom-call | tf_op jit(solution)/shard_map/gate/pallas_call | solution.py:454
  3.9 0.0 copy-start
  4.0 7.3 %all-to-all-start = ((bf16[32,104,128]{2,1,0:T(8,128)(2,1)}), bf16[32,104,128]{2,1,0:T(8,128)(2,1)S(1)}, u32[]{:S(2)}, u32[]{:S(2)}) async-start(bf16[32,104,128]{2,1,0:T(8,128)(2,1)} %gate.1), calls=%async_computation | async-start | bytes 1703936 | tf_op jit(solution)/shard_map/all_to_all | solution.py:471
  11.3 0.0 copy-done.3
  11.3 0.1 reshape.26
  11.4 0.1 dynamic-slice_reduce_fusion.2
  11.5 0.1 slice.19
  11.6 0.1 slice.21
  11.7 0.1 slice.23
  11.8 0.2 copy.16
  11.9 0.1 reshape.28
  12.0 2.8 %prepare.1 = (f32[3,128,1024]{2,1,0:T(8,128)}, f32[3,8,1024]{2,1,0:T(8,128)}, f32[8,128]{1,0:T(8,128)}) custom-call(bf16[128,1024]{1,0:T(8,128)(2,1)} %q_ref.1, bf16[128,1024]{1,0:T(8,128)(2,1)} %k_ref.1, bf16[128,1024]{1,0:T(8,128)(2,1)} %v_ref.1, f32[3,3,1024]{2,1,0:T(4,128)} %taps_ref.3), custom_call_target="tpu_custom_call" | custom-call | flops 3932160 | bytes 2621440 | tf_op jit(solution)/shard_map/prepare/pallas_call | solution.py:472
  14.8 0.7 %broadcast_multiply_fusion.own_ref = f32[3,8,128]{2,1,0:T(8,128)S(1)} fusion(f32[3,8,128]{2,1,0:T(8,128)S(1)} %reshape.28, f32[8,128]{1,0:T(8,128)} %get-tuple-element.7), kind=kLoop, calls=%fused_computation.1 | loop fusion | flops 3072 | bytes 28672 | tf_op jit(solution)/shard_map/mul | solution.py:491
  15.5 0.0 copy-start.2
  15.5 0.0 copy-start.4
  15.5 0.0 copy-start.5
  15.5 0.0 copy-start.6
  15.6 17.7 %all-to-all-done.x_ref = bf16[32,104,128]{2,1,0:T(8,128)(2,1)S(1)} async-done(((bf16[32,104,128]{2,1,0:T(8,128)(2,1)}), bf16[32,104,128]{2,1,0:T(8,128)(2,1)S(1)}, u32[]{:S(2)}, u32[]{:S(2)}) %all-to-all-start) | async-done | bytes 852000 | tf_op jit(solution)/shard_map/all_to_all | solution.py:471
  33.3 0.0 copy-done
  33.3 0.0 copy-start.1
  33.3 5.7 %transform.1 = bf16[32,72,128]{2,1,0:T(8,128)(2,1)S(1)} custom-call(bf16[32,104,128]{2,1,0:T(8,128)(2,1)S(1)} %all-to-all-done.x_ref, f32[3,8,128]{2,1,0:T(8,128)S(1)} %broadcast_multiply_fusion.own_ref, bf16[3584,256]{1,0:T(8,128)(2,1)S(1)} %copy-done), custom_call_target="tpu_custom_call" | custom-call | tf_op jit(solution)/shard_map/transform/pallas_call | solution.py:485
  39.0 20.2 %all_to_all.10.y_ref = bf16[32,72,128]{2,1,0:T(8,128)(2,1)S(1)} all-to-all(bf16[32,72,128]{2,1,0:T(8,128)(2,1)S(1)} %transform.1), channel_id=1, replica_groups=mesh['outer'=8,'inner'=4] {'outer','inner'}, dimensions={0} | all-to-all | bytes 1179648 | tf_op jit(solution)/shard_map/all_to_all | solution.py:492
  59.2 0.0 copy-done.2
  59.2 0.0 copy-done.4
  59.2 0.0 copy-done.5
  59.2 0.0 copy-done.6
  59.2 0.0 copy-done.1
  59.2 2.2 %finish.1 = (bf16[128,1024]{1,0:T(8,128)(2,1)}, bf16[128,1024]{1,0:T(8,128)(2,1)}, bf16[128,1024]{1,0:T(8,128)(2,1)}, bf16[128,1024]{1,0:T(8,128)(2,1)}) custom-call(bf16[32,72,128]{2,1,0:T(8,128)(2,1)S(1)} %all_to_all.10.y_ref, bf16[128,1024]{1,0:T(8,128)(2,1)S(1)} %copy-done.2, f32[3,128,1024]{2,1,0:T(8,128)S(1)} %copy-done.1, ...), custom_call_target="tpu_custom_call" | custom-call | tf_op jit(solution)/shard_map/finish/pallas_call | solution.py:494
  (4 shorter events, 0.0 us)
Async XLA Ops:
  0.6 10.6 %copy-start.3 = (f32[3,3,1024]{2,1,0:T(4,128)S(1)}, f32[3,3,1024]{2,1,0:T(4,128)}, u32[]{:S(2)}) copy-start(f32[3,3,1024]{2,1,0:T(4,128)} %taps_ref.3) | copy-start | bytes 110596
  3.9 29.4 %copy-start = (bf16[3584,256]{1,0:T(8,128)(2,1)S(1)}, bf16[3584,256]{1,0:T(8,128)(2,1)}, u32[]{:S(2)}) copy-start(bf16[3584,256]{1,0:T(8,128)(2,1)} %constant.22.clone.table_ref) | copy-start | bytes 5505028
  4.0 29.3 %all-to-all-start = ((bf16[32,104,128]{2,1,0:T(8,128)(2,1)}), bf16[32,104,128]{2,1,0:T(8,128)(2,1)S(1)}, u32[]{:S(2)}, u32[]{:S(2)}) async-start(bf16[32,104,128]{2,1,0:T(8,128)(2,1)} %gate.1), calls=%async_computation | async-start | bytes 1703936 | tf_op jit(solution)/shard_map/all_to_all | solution.py:471
  15.5 43.6 %copy-start.2 = (bf16[128,1024]{1,0:T(8,128)(2,1)S(1)}, bf16[128,1024]{1,0:T(8,128)(2,1)}, u32[]{:S(2)}) copy-start(bf16[128,1024]{1,0:T(8,128)(2,1)} %g_ref.1) | copy-start | bytes 786436
  15.5 43.6 %copy-start.4 = (f32[3,3,1024]{2,1,0:T(4,128)S(1)}, f32[3,3,1024]{2,1,0:T(4,128)}, u32[]{:S(2)}) copy-start(f32[3,3,1024]{2,1,0:T(4,128)} %taps_ref.3) | copy-start | bytes 110596
  15.5 43.6 %copy-start.5 = (f32[3,8,1024]{2,1,0:T(8,128)S(1)}, f32[3,8,1024]{2,1,0:T(8,128)}, u32[]{:S(2)}) copy-start(f32[3,8,1024]{2,1,0:T(8,128)} %get-tuple-element.9.tail_ref) | copy-start | bytes 294916
  15.5 43.6 %copy-start.6 = (f32[1024]{0:T(1024)S(1)}, f32[1024]{0:T(1024)}, u32[]{:S(2)}) copy-start(f32[1024]{0:T(1024)} %param.13) | copy-start | bytes 12292
  33.3 25.9 %copy-start.1 = (f32[3,128,1024]{2,1,0:T(8,128)S(1)}, f32[3,128,1024]{2,1,0:T(8,128)}, u32[]{:S(2)}) copy-start(f32[3,128,1024]{2,1,0:T(8,128)} %get-tuple-element.8.short_ref) | copy-start | bytes 4718596

commit v4 on v3

--- a/solution.py
+++ b/solution.py
@@ -46,9 +46,8 @@
     return high, low
 
 
-def table_on_left(high_table, low_table, value):
+def table_on_left(table, value):
     high, low = split_pair(value)
-    table = jnp.concatenate([high_table, high_table, low_table], axis=1)
     return jnp.dot(table, jnp.concatenate([high, low, high], axis=0), preferred_element_type=f32)
 
 
@@ -61,40 +60,89 @@
 @functools.lru_cache(maxsize=None)
 def tables(blocks, rows, unit):
     points = 2 * blocks * rows
-    bins = np.arange(blocks) + 0.5
-    angle = np.outer(bins, np.arange(blocks)) * (2 * math.pi / (2 * blocks))
+    bins = 2 * np.arange(blocks // 4) + 1
     eye = np.eye(unit)
-    coarse = np.concatenate([np.kron(np.cos(angle), eye), np.kron(-np.sin(angle), eye)], axis=0)
-    coarse_back = np.concatenate(
-        [np.kron(np.cos(angle).T, eye), np.kron(-np.sin(angle).T, eye)], axis=1
-    ) * (2.0 / points)
-    twist = np.repeat(np.outer(bins, np.arange(rows)) * (2 * math.pi / points), unit, axis=0)
+    coarse, coarse_back = [], []
+    for which in range(4):
+        angle = np.outer(bins, np.arange(which, blocks, 4)) * (math.pi / (2 * blocks))
+        parts = [np.kron(np.cos(angle), eye), np.kron(-np.sin(angle), eye)]
+        coarse.append(np.concatenate(parts, axis=0))
+        coarse_back.append(np.concatenate([part.T for part in parts], axis=1) * (2.0 / points))
+    signed = np.concatenate([bins, blocks + bins, bins - blocks, bins - 2 * blocks])
+    twist = np.repeat(np.outer(signed, np.arange(rows)) * (math.pi / points), unit, axis=0)
     fine = np.outer(np.arange(rows), np.arange(rows)) * (2 * math.pi / rows)
     cos, sin = np.cos(fine), np.sin(fine)
     forward = np.block([[cos, -sin], [sin, cos]])
     backward = np.block([[cos, sin], [-sin, cos]])
-    columns = 2 * rows
     twists = np.concatenate([np.cos(twist), np.sin(twist)], axis=1)
-    flat = []
-    for table in (coarse, coarse_back, forward, backward, twists):
-        for half in numpy_pair(table):
-            flat += np.split(half, table.shape[1] // columns, axis=1)
+    whole = []
+    for table in coarse + coarse_back:
+        high, low = numpy_pair(table)
+        whole.append(np.concatenate([high, high, low], axis=1))
+    for table in (forward, backward, twists):
+        whole += numpy_pair(table)
+    columns, flat = 2 * rows, []
+    for table in whole:
+        wide = np.pad(table, ((0, 0), (0, -table.shape[1] % columns)))
+        flat += np.split(wide, wide.shape[1] // columns, axis=1)
     return np.concatenate(flat)
 
 
 def unpack_tables(ref, count, rows):
-    columns = 2 * rows
-    shapes = [(2 * count, count)] * 2 + [(count, 2 * count)] * 2 + [(columns, columns)] * 4
-    shapes += [(count, columns)] * 2
+    columns, quarter = 2 * rows, count // 4
+    shapes = [(2 * quarter, 3 * quarter)] * 4 + [(quarter, 6 * quarter)] * 4
+    shapes += [(columns, columns)] * 4 + [(count, columns)] * 2
     found, at = [], 0
     for height, length in shapes:
         parts = []
-        for _ in range(length // columns):
-            parts.append(ref[at : at + height])
+        for start in range(0, length, columns):
+            parts.append(ref[at : at + height, : min(columns, length - start)])
             at += height
         found.append(jnp.concatenate(parts, axis=1) if len(parts) > 1 else parts[0])
-    twists = found[8].astype(f32) + found[9].astype(f32)
-    return found[0:2], found[2:4], found[4:6], found[6:8], twists[:, :rows], twists[:, rows:]
+    twists = found[12].astype(f32) + found[13].astype(f32)
+    return found[:4], found[4:8], found[8:10], found[10:12], twists[:, :rows], twists[:, rows:]
+
+
+def coarse_forward(coarse, value, blocks, unit):
+    sums = []
+    for which in range(4):
+        places = range(which * unit, blocks * unit, 4 * unit)
+        part = jnp.concatenate([value[at : at + unit] for at in places], axis=0)
+        total = table_on_left(coarse[which], part)
+        half = total.shape[0] // 2
+        sums.append((total[:half], total[half:]))
+    even = [left + right for left, right in zip(sums[0], sums[2])]
+    even_less = [left - right for left, right in zip(sums[0], sums[2])]
+    odd = [left + right for left, right in zip(sums[1], sums[3])]
+    odd_less = [left - right for left, right in zip(sums[1], sums[3])]
+    real = [even[0] + odd[0], even_less[0] + odd_less[1], even_less[0] - odd_less[1], even[0] - odd[0]]
+    imag = [even[1] + odd[1], even_less[1] - odd_less[0], even_less[1] + odd_less[0], even[1] - odd[1]]
+    return jnp.concatenate(real, axis=0), jnp.concatenate(imag, axis=0)
+
+
+def coarse_backward(coarse_back, real, imag, blocks, unit):
+    quarter = blocks * unit // 4
+    real = [real[at * quarter : (at + 1) * quarter] for at in range(4)]
+    imag = [imag[at * quarter : (at + 1) * quarter] for at in range(4)]
+    outer_real, outer_imag = real[0] + real[3], imag[0] + imag[3]
+    inner_real, inner_imag = real[1] + real[2], imag[1] + imag[2]
+    outer_real_less, outer_imag_less = real[0] - real[3], imag[0] - imag[3]
+    inner_real_less, inner_imag_less = real[1] - real[2], imag[1] - imag[2]
+    mixes = (
+        (outer_real + inner_real, outer_imag + inner_imag),
+        (outer_real_less - inner_imag_less, outer_imag_less + inner_real_less),
+        (outer_real - inner_real, outer_imag - inner_imag),
+        (outer_real_less + inner_imag_less, outer_imag_less - inner_real_less),
+    )
+    results = [
+        table_on_left(coarse_back[which], jnp.concatenate(mix, axis=0))
+        for which, mix in enumerate(mixes)
+    ]
+    pieces = []
+    for block in range(blocks):
+        at = block // 4 * unit
+        pieces.append(results[block % 4][at : at + unit])
+    return jnp.concatenate(pieces, axis=0)
 
 
 def shifted(stream, steps, rim):
@@ -278,13 +326,13 @@
         stacked = jnp.concatenate(
             [taken[which][at] for at in range(together) for which in range(3)], axis=1
         )
-        first = table_on_left(*coarse, stacked)
+        first_real, first_imag = coarse_forward(coarse, stacked, blocks, unit)
         lasts = []
         for at in range(together):
             spectra = []
             for which in range(3):
                 here = slice((3 * at + which) * rows, (3 * at + which + 1) * rows)
-                real, imag = first[:count, here], first[count:, here]
+                real, imag = first_real[:, here], first_imag[:, here]
                 turned = jnp.concatenate(
                     [real * cos + imag * sin, imag * cos - real * sin], axis=1
                 )
@@ -298,10 +346,9 @@
                 product = jnp.concatenate([real, imag], axis=1)
                 plain = table_on_right(product, *backward)
                 real, imag = plain[:, :rows], plain[:, rows:]
-                lasts.append(
-                    jnp.concatenate([real * cos - imag * sin, imag * cos + real * sin], axis=0)
-                )
-        result = table_on_left(*coarse_back, jnp.concatenate(lasts, axis=1))
+                lasts.append((real * cos - imag * sin, imag * cos + real * sin))
+        real, imag = (jnp.concatenate(parts, axis=1) for parts in zip(*lasts))
+        result = coarse_backward(coarse_back, real, imag, blocks, unit)
         for which in range(2):
             pieces = []
             for at in range(together):
@@ -327,7 +374,7 @@
     out_ref[:, 2 * width :, :] = lines.reshape(blocks, unit, rows).astype(bf16)
 
 
-def prepare_kernel(q_ref, k_ref, v_ref, taps_ref, short_ref, tail_ref, ready_ref):
+def prepare_kernel(q_ref, k_ref, v_ref, taps_ref, sq_ref, skv_ref, tail_ref, ready_ref):
     rows, channels = q_ref.shape
     chunk = 128
     none = jnp.zeros((2, chunk), f32)
@@ -337,13 +384,12 @@
         for which, ref in enumerate((q_ref, k_ref, v_ref)):
             stream = ref[:, lanes].astype(f32)
             tail_ref[which, :, lanes] = stream[rows - 8 :]
-            short_ref[which, :, lanes] = short_forward(
-                stream, taps_at(taps_ref, which, lanes), none
-            )
+            target = sq_ref if which == 0 else skv_ref.at[which - 1]
+            target[:, lanes] = short_forward(stream, taps_at(taps_ref, which, lanes), none)
 
 
 def finish_kernel(
-    unit, y_ref, g_ref, short_ref, tail_ref, taps_ref, skip_ref, *refs
+    unit, y_ref, g_ref, sq_ref, skv_ref, tail_ref, taps_ref, skip_ref, *refs
 ):
     targets, held, sems = refs[:4], refs[4:8], refs[8]
     rows, channels = g_ref.shape
@@ -384,7 +430,7 @@
         for which, at in ((0, 2), (1, 0), (2, 1)):
             one, two, three = taps[which]
             past = before[at]
-            short = short_ref[which, :, lanes]
+            short = sq_ref[:, lanes] if which == 0 else skv_ref[which - 1, :, lanes]
             edge = short[:8] + jnp.where(
                 row == 0,
                 two * past[1:2] + three * past[0:1],
@@ -469,10 +515,11 @@
         name="gate",
     )(query_in, key_in, value_in, grad_out, long_filter, conv_taps)
     spread = lax.all_to_all(packed, AXES, 0, 0, tiled=True)
-    short, tail, ready = pl.pallas_call(
+    *short, tail, ready = pl.pallas_call(
         prepare_kernel,
         out_shape=(
-            jax.ShapeDtypeStruct((3, rows, channels), f32),
+            jax.ShapeDtypeStruct((rows, channels), f32),
+            jax.ShapeDtypeStruct((2, rows, channels), f32),
             jax.ShapeDtypeStruct((3, 8, channels), f32),
             jax.ShapeDtypeStruct((unit, rows), f32),
         ),
@@ -494,12 +541,12 @@
     return pl.pallas_call(
         functools.partial(finish_kernel, unit),
         out_shape=(wide, wide, wide, wide),
-        in_specs=[near] * 6,
+        in_specs=[near] * 7,
         out_specs=(far, far, far, far),
         scratch_shapes=[*[stream] * 4, pltpu.SemaphoreType.DMA((parts, 4))],
         compiler_params=small,
         name="finish",
-    )(returned, grad_out, short, tail, conv_taps, skip)
+    )(returned, grad_out, *short, tail, conv_taps, skip)
 
 
 def solution(mesh):

time: 61.6 us -> 61 us (level)
  Pallas kernels: 13.9 us -> 13.2 us
    pallas_call x1, Pallas kernels: 5.69 us -> 5.06 us  [local(): pl.pallas_call(functools.partial(transform_kernel, groups, width), out_sh...]
  transfers between devices with their start and end apart: 1 -> 1, of which waited for: 1 -> 1; matrix products, arithmetic and copies ran while one was open for 2% -> 2% of each run, Pallas kernels for 5% -> 4%
where the time goes in v4:
time: 61 us; the launch traced here: 60.7 us
  blocking collectives  20.2 us (33%)
  waiting for transfers between devices  17.9 us (29%)
  Pallas kernels  13.2 us (22%)
  starting transfers between devices  7.3 us (12%)
  between operations  0.76 us (1%)
  local copies, waits for them, and re-layouts  0.75 us (1%)
  other arithmetic  0.7 us (1%)
    all_to_all x1, blocking collectives, local(): returned = lax.all_to_all(result, AXES, 0, 0, tiled=True)  20.2 us
    all_to_all x1, waiting for transfers between devices, local(): spread = lax.all_to_all(packed, AXES, 0, 0, tiled=True)  17.9 us
    all_to_all x1, starting transfers between devices, local(): spread = lax.all_to_all(packed, AXES, 0, 0, tiled=True)  7.3 us
    pallas_call x1, Pallas kernels, local(): pl.pallas_call(functools.partial(transform_kernel, groups, width), out_sh...  5.06 us
    pallas_call x1, Pallas kernels, local(): pl.pallas_call(functools.partial(gate_kernel, unit), out_shape=jax.ShapeD...  3.31 us
    pallas_call x1, Pallas kernels, local(): pl.pallas_call(prepare_kernel, out_shape=(jax.ShapeDtypeStruct((rows, cha...  2.65 us
    pallas_call x1, Pallas kernels, local(): pl.pallas_call(functools.partial(finish_kernel, unit), out_shape=(wide, w...  2.15 us
  transfers between devices with their start and end apart: 1, of which 1 were waited for; matrix products, arithmetic and copies ran while one was open for 2% of the time, Pallas kernels for 4%

profile of v4, /device:TPU:0, one launch (start us, length us, event | category | flops | bytes accessed | tf_op | source)
XLA Modules:
  0.0 60.7 jit_solution(9132963445556896462)
XLA Ops:
  0.6 3.3 %gate.1 = bf16[32,104,128]{2,1,0:T(8,128)(2,1)} custom-call(bf16[128,1024]{1,0:T(8,128)(2,1)} %q_ref.1, bf16[128,1024]{1,0:T(8,128)(2,1)} %k_ref.1, bf16[128,1024]{1,0:T(8,128)(2,1)} %v_ref.1, bf16[128,1024]{1,0:T(8,128)(2,1)} %g_ref.1, f32[128,1024]{1,0:T(8,128)} %h_hbm.1, f32[3,3,1024]{2,1,0:T(4,128)} %taps_ref.3), custom_call_target="tpu_custom_call" | custom-call | tf_op jit(solution)/shard_map/gate/pallas_call | solution.py:500
  4.0 0.0 copy-start.3
  4.0 0.0 copy-start
  4.0 7.3 %all-to-all-start = ((bf16[32,104,128]{2,1,0:T(8,128)(2,1)}), bf16[32,104,128]{2,1,0:T(8,128)(2,1)S(1)}, u32[]{:S(2)}, u32[]{:S(2)}) async-start(bf16[32,104,128]{2,1,0:T(8,128)(2,1)} %gate.1), calls=%async_computation | async-start | bytes 1703936 | tf_op jit(solution)/shard_map/all_to_all | solution.py:517
  11.3 0.0 copy-done.3
  11.3 0.1 reshape.26
  11.5 0.1 dynamic-slice_reduce_fusion.2
  11.5 0.1 slice.19
  11.6 0.1 slice.21
  11.7 0.1 slice.23
  11.8 0.2 copy.16
  12.0 0.1 reshape.28
  12.1 2.7 %prepare.1 = (f32[128,1024]{1,0:T(8,128)}, f32[2,128,1024]{2,1,0:T(8,128)}, f32[3,8,1024]{2,1,0:T(8,128)}, f32[8,128]{1,0:T(8,128)}) custom-call(bf16[128,1024]{1,0:T(8,128)(2,1)} %q_ref.1, bf16[128,1024]{1,0:T(8,128)(2,1)} %k_ref.1, bf16[128,1024]{1,0:T(8,128)(2,1)} %v_ref.1, f32[3,3,1024]{2,1,0:T(4,128)} %taps_ref.3), custom_call_target="tpu_custom_call" | custom-call | flops 3932160 | bytes 2621440 | tf_op jit(solution)/shard_map/prepare/pallas_call | solution.py:518
  14.7 0.7 %broadcast_multiply_fusion.own_ref = f32[3,8,128]{2,1,0:T(8,128)S(1)} fusion(f32[3,8,128]{2,1,0:T(8,128)S(1)} %reshape.28, f32[8,128]{1,0:T(8,128)} %get-tuple-element.8), kind=kLoop, calls=%fused_computation.1 | loop fusion | flops 3072 | bytes 28672 | tf_op jit(solution)/shard_map/mul | solution.py:538
  15.4 0.0 copy-start.1
  15.4 0.0 copy-start.2
  15.4 0.0 copy-start.4
  15.4 0.0 copy-start.7
  15.4 17.9 %all-to-all-done.x_ref = bf16[32,104,128]{2,1,0:T(8,128)(2,1)S(1)} async-done(((bf16[32,104,128]{2,1,0:T(8,128)(2,1)}), bf16[32,104,128]{2,1,0:T(8,128)(2,1)S(1)}, u32[]{:S(2)}, u32[]{:S(2)}) %all-to-all-start) | async-done | bytes 852000 | tf_op jit(solution)/shard_map/all_to_all | solution.py:517
  33.3 0.0 copy-done
  33.3 0.0 copy-start.5
  33.3 0.0 copy-start.6
  33.3 5.1 %transform.1 = bf16[32,72,128]{2,1,0:T(8,128)(2,1)S(1)} custom-call(bf16[32,104,128]{2,1,0:T(8,128)(2,1)S(1)} %all-to-all-done.x_ref, f32[3,8,128]{2,1,0:T(8,128)S(1)} %broadcast_multiply_fusion.own_ref, bf16[2560,256]{1,0:T(8,128)(2,1)S(1)} %copy-done), custom_call_target="tpu_custom_call" | custom-call | tf_op jit(solution)/shard_map/transform/pallas_call | solution.py:532
  38.4 20.2 %all_to_all.10.y_ref = bf16[32,72,128]{2,1,0:T(8,128)(2,1)S(1)} all-to-all(bf16[32,72,128]{2,1,0:T(8,128)(2,1)S(1)} %transform.1), channel_id=1, replica_groups=mesh['outer'=8,'inner'=4] {'outer','inner'}, dimensions={0} | all-to-all | bytes 1179648 | tf_op jit(solution)/shard_map/all_to_all | solution.py:539
  58.5 0.0 copy-done.1
  58.6 0.0 copy-done.2
  58.6 0.0 copy-done.4
  58.6 0.0 copy-done.7
  58.6 0.0 copy-done.5
  58.6 0.0 copy-done.6
  58.6 2.2 %finish.1 = (bf16[128,1024]{1,0:T(8,128)(2,1)}, bf16[128,1024]{1,0:T(8,128)(2,1)}, bf16[128,1024]{1,0:T(8,128)(2,1)}, bf16[128,1024]{1,0:T(8,128)(2,1)}) custom-call(bf16[32,72,128]{2,1,0:T(8,128)(2,1)S(1)} %all_to_all.10.y_ref, bf16[128,1024]{1,0:T(8,128)(2,1)S(1)} %copy-done.2, f32[128,1024]{1,0:T(8,128)S(1)} %copy-done.5, f32[2,128,1024]{2,1,0:T(8,128)S(1)} %copy-done.1, ...), custom_call_target="tpu_custom_call" | custom-call | tf_op jit(solution)/shard_map/finish/pallas_call | solution.py:541
  (4 shorter events, 0.0 us)
Async XLA Ops:
  4.0 7.3 %copy-start.3 = (f32[3,3,1024]{2,1,0:T(4,128)S(1)}, f32[3,3,1024]{2,1,0:T(4,128)}, u32[]{:S(2)}) copy-start(f32[3,3,1024]{2,1,0:T(4,128)} %taps_ref.3) | copy-start | bytes 110596
  4.0 29.4 %copy-start = (bf16[2560,256]{1,0:T(8,128)(2,1)S(1)}, bf16[2560,256]{1,0:T(8,128)(2,1)}, u32[]{:S(2)}) copy-start(bf16[2560,256]{1,0:T(8,128)(2,1)} %constant.22.clone.table_ref) | copy-start | bytes 3932164
  4.0 29.3 %all-to-all-start = ((bf16[32,104,128]{2,1,0:T(8,128)(2,1)}), bf16[32,104,128]{2,1,0:T(8,128)(2,1)S(1)}, u32[]{:S(2)}, u32[]{:S(2)}) async-start(bf16[32,104,128]{2,1,0:T(8,128)(2,1)} %gate.1), calls=%async_computation | async-start | bytes 1703936 | tf_op jit(solution)/shard_map/all_to_all | solution.py:517
  15.4 43.2 %copy-start.1 = (f32[2,128,1024]{2,1,0:T(8,128)S(1)}, f32[2,128,1024]{2,1,0:T(8,128)}, u32[]{:S(2)}) copy-start(f32[2,128,1024]{2,1,0:T(8,128)} %get-tuple-element.10.skv_ref) | copy-start | bytes 3145732
  15.4 43.2 %copy-start.2 = (bf16[128,1024]{1,0:T(8,128)(2,1)S(1)}, bf16[128,1024]{1,0:T(8,128)(2,1)}, u32[]{:S(2)}) copy-start(bf16[128,1024]{1,0:T(8,128)(2,1)} %g_ref.1) | copy-start | bytes 786436
  15.4 43.2 %copy-start.4 = (f32[3,3,1024]{2,1,0:T(4,128)S(1)}, f32[3,3,1024]{2,1,0:T(4,128)}, u32[]{:S(2)}) copy-start(f32[3,3,1024]{2,1,0:T(4,128)} %taps_ref.3) | copy-start | bytes 110596
  15.4 43.2 %copy-start.7 = (f32[1024]{0:T(1024)S(1)}, f32[1024]{0:T(1024)}, u32[]{:S(2)}) copy-start(f32[1024]{0:T(1024)} %param.13) | copy-start | bytes 12292
  33.3 25.3 %copy-start.5 = (f32[128,1024]{1,0:T(8,128)S(1)}, f32[128,1024]{1,0:T(8,128)}, u32[]{:S(2)}) copy-start(f32[128,1024]{1,0:T(8,128)} %get-tuple-element.9.sq_ref) | copy-start | bytes 1572868
  33.3 25.3 %copy-start.6 = (f32[3,8,1024]{2,1,0:T(8,128)S(1)}, f32[3,8,1024]{2,1,0:T(8,128)}, u32[]{:S(2)}) copy-start(f32[3,8,1024]{2,1,0:T(8,128)} %get-tuple-element.11.tail_ref) | copy-start | bytes 294916

commit v5 on v4

--- a/solution.py
+++ b/solution.py
@@ -180,7 +180,7 @@
 
 
 def slices_of(channels):
-    size = min(256, channels)
+    size = min(512, channels)
     return [pl.ds(start, size) for start in range(0, channels, size)]
 
 
@@ -192,7 +192,6 @@
     run = min(width, 2 * unit)
     span = run * blocks
     chunk = 128
-    starts = range(0, channels, chunk)
     pairs = (
         (taps_hbm, taps_ref),
         (k_hbm, k_ref),
@@ -230,50 +229,47 @@
             words = words.T.reshape(chunk // run, run, rows).astype(bf16)
         out_ref[pl.ds(first, chunk // run), pl.ds(which * width + line, run), :] = words
 
+    halves = run // unit
+    waited = []
+
+    def wait_for(*which):
+        for at in which:
+            if at not in waited:
+                copies[at].wait()
+                waited.append(at)
+
     outs = []
-
-    def leave(at, first, count):
-        if run % 16 == 0:
-            part = (slice(None), pl.ds(first, count))
-            copy = pltpu.make_async_copy(out_ref.at[part], out_hbm.at[part], out_sems.at[at])
-            copy.start()
-            outs.append(copy)
-
-    for copy in copies[:3]:
-        copy.wait()
-    for start in starts:
-        lanes = pl.ds(start, chunk)
-        send(0, start, short(k_ref, 1, 0, lanes) * short(v_ref, 2, 1, lanes))
-    leave(0, 0, width)
-    copies[3].wait()
-    copies[4].wait()
-    for start in starts:
-        lanes = pl.ds(start, chunk)
-        upstream = g_ref[:, lanes].astype(f32)
-        extra[6:8, lanes] = upstream[0:2]
-        send(2, start, upstream * short(q_ref, 0, 2, lanes))
-    leave(2, 2 * width, width)
-    copies[5].wait()
-    for start in starts:
-        send(1, start, h_ref[:, pl.ds(start, chunk)])
-    leave(1, width, width)
-    halves = run // unit
-    items = []
-    for start in range(0, channels, span):
-        items += [extra[:, start : start + span]] * halves
-    if ITEMS * len(items) < rows:
-        items.append(jnp.zeros((rows - ITEMS * len(items), span), f32))
-    lines = jnp.concatenate(items, axis=0).T.reshape(blocks, run, rows)
-    lane = lax.broadcasted_iota(jnp.int32, (blocks, unit, rows), 2)
-    merged = lines[:, :unit, :]
-    for half in range(1, halves):
-        part = lines[:, half * unit : (half + 1) * unit, :]
-        merged = jnp.where(lane // ITEMS % halves == half, part, merged)
-    out_ref[:, 3 * width :, :] = merged.astype(bf16)
-    if run % 16 == 0:
-        leave(3, 3 * width, unit)
-    else:
-        copy = pltpu.make_async_copy(out_ref, out_hbm, out_sems.at[0])
+    for part in range(2):
+        half_span = span // 2
+        firsts = [at + part * half_span for at in range(0, channels, span)]
+        starts = [first + at for first in firsts for at in range(0, half_span, chunk)]
+        wait_for(0, 1, 2)
+        for start in starts:
+            lanes = pl.ds(start, chunk)
+            send(0, start, short(k_ref, 1, 0, lanes) * short(v_ref, 2, 1, lanes))
+        wait_for(3, 4)
+        for start in starts:
+            lanes = pl.ds(start, chunk)
+            upstream = g_ref[:, lanes].astype(f32)
+            extra[6:8, lanes] = upstream[0:2]
+            send(2, start, upstream * short(q_ref, 0, 2, lanes))
+        wait_for(5)
+        for start in starts:
+            send(1, start, h_ref[:, pl.ds(start, chunk)])
+        items = []
+        for first in firsts:
+            items += [extra[:, first : first + half_span]] * halves
+        if ITEMS * len(items) < rows:
+            items.append(jnp.zeros((rows - ITEMS * len(items), half_span), f32))
+        lines = jnp.concatenate(items, axis=0).T.reshape(blocks // 2, run, rows)
+        lane = lax.broadcasted_iota(jnp.int32, (blocks // 2, unit, rows), 2)
+        merged = lines[:, :unit, :]
+        for half in range(1, halves):
+            other = lines[:, half * unit : (half + 1) * unit, :]
+            merged = jnp.where(lane // ITEMS % halves == half, other, merged)
+        mine = pl.ds(part * (blocks // 2), blocks // 2)
+        out_ref[mine, 3 * width :, :] = merged.astype(bf16)
+        copy = pltpu.make_async_copy(out_ref.at[mine], out_hbm.at[mine], out_sems.at[part])
         copy.start()
         outs.append(copy)
     for copy in outs:
@@ -509,7 +505,7 @@
             pltpu.VMEM((blocks, 3 * width + unit, rows), bf16),
             pltpu.VMEM((ITEMS, channels), f32),
             pltpu.SemaphoreType.DMA((6,)),
-            pltpu.SemaphoreType.DMA((4,)),
+            pltpu.SemaphoreType.DMA((2,)),
         ],
         compiler_params=large,
         name="gate",

time: 61 us -> 60.9 us (level)
  no operation moved by 1% of the time
where the time goes in v5:
time: 60.9 us; the launch traced here: 60.7 us
  blocking collectives  20.2 us (33%)
  waiting for transfers between devices  17.9 us (29%)
  Pallas kernels  13.1 us (22%)
  starting transfers between devices  7.3 us (12%)
  between operations  0.76 us (1%)
  local copies, waits for them, and re-layouts  0.75 us (1%)
  other arithmetic  0.7 us (1%)
    all_to_all x1, blocking collectives, local(): returned = lax.all_to_all(result, AXES, 0, 0, tiled=True)  20.2 us
    all_to_all x1, waiting for transfers between devices, local(): spread = lax.all_to_all(packed, AXES, 0, 0, tiled=True)  17.9 us
    all_to_all x1, starting transfers between devices, local(): spread = lax.all_to_all(packed, AXES, 0, 0, tiled=True)  7.3 us
    pallas_call x1, Pallas kernels, local(): pl.pallas_call(functools.partial(transform_kernel, groups, width), out_sh...  5.06 us
    pallas_call x1, Pallas kernels, local(): pl.pallas_call(functools.partial(gate_kernel, unit), out_shape=jax.ShapeD...  3.3 us
    pallas_call x1, Pallas kernels, local(): pl.pallas_call(prepare_kernel, out_shape=(jax.ShapeDtypeStruct((rows, cha...  2.65 us
    pallas_call x1, Pallas kernels, local(): pl.pallas_call(functools.partial(finish_kernel, unit), out_shape=(wide, w...  2.1 us
  transfers between devices with their start and end apart: 1, of which 1 were waited for; matrix products, arithmetic and copies ran while one was open for 2% of the time, Pallas kernels for 4%

profile of v5, /device:TPU:0, one launch (start us, length us, event | category | flops | bytes accessed | tf_op | source)
XLA Modules:
  0.0 60.7 jit_solution(3673217209413425189)
XLA Ops:
  0.6 3.3 %gate.1 = bf16[32,104,128]{2,1,0:T(8,128)(2,1)} custom-call(bf16[128,1024]{1,0:T(8,128)(2,1)} %q_ref.1, bf16[128,1024]{1,0:T(8,128)(2,1)} %k_ref.1, bf16[128,1024]{1,0:T(8,128)(2,1)} %v_ref.1, bf16[128,1024]{1,0:T(8,128)(2,1)} %g_ref.1, f32[128,1024]{1,0:T(8,128)} %h_hbm.1, f32[3,3,1024]{2,1,0:T(4,128)} %taps_ref.3), custom_call_target="tpu_custom_call" | custom-call | tf_op jit(solution)/shard_map/gate/pallas_call | solution.py:496
  3.9 0.0 copy-start.3
  4.0 0.0 copy-start
  4.0 7.3 %all-to-all-start = ((bf16[32,104,128]{2,1,0:T(8,128)(2,1)}), bf16[32,104,128]{2,1,0:T(8,128)(2,1)S(1)}, u32[]{:S(2)}, u32[]{:S(2)}) async-start(bf16[32,104,128]{2,1,0:T(8,128)(2,1)} %gate.1), calls=%async_computation | async-start | bytes 1703936 | tf_op jit(solution)/shard_map/all_to_all | solution.py:513
  11.3 0.0 copy-done.3
  11.3 0.1 reshape.26
  11.4 0.1 dynamic-slice_reduce_fusion.2
  11.5 0.1 slice.19
  11.6 0.1 slice.21
  11.7 0.1 slice.23
  11.8 0.2 copy.16
  12.0 0.1 reshape.28
  12.0 2.7 %prepare.1 = (f32[128,1024]{1,0:T(8,128)}, f32[2,128,1024]{2,1,0:T(8,128)}, f32[3,8,1024]{2,1,0:T(8,128)}, f32[8,128]{1,0:T(8,128)}) custom-call(bf16[128,1024]{1,0:T(8,128)(2,1)} %q_ref.1, bf16[128,1024]{1,0:T(8,128)(2,1)} %k_ref.1, bf16[128,1024]{1,0:T(8,128)(2,1)} %v_ref.1, f32[3,3,1024]{2,1,0:T(4,128)} %taps_ref.3), custom_call_target="tpu_custom_call" | custom-call | flops 3932160 | bytes 2621440 | tf_op jit(solution)/shard_map/prepare/pallas_call | solution.py:514
  14.7 0.7 %broadcast_multiply_fusion.own_ref = f32[3,8,128]{2,1,0:T(8,128)S(1)} fusion(f32[3,8,128]{2,1,0:T(8,128)S(1)} %reshape.28, f32[8,128]{1,0:T(8,128)} %get-tuple-element.8), kind=kLoop, calls=%fused_computation.1 | loop fusion | flops 3072 | bytes 28672 | tf_op jit(solution)/shard_map/mul | solution.py:534
  15.4 0.0 copy-start.1
  15.4 0.0 copy-start.2
  15.4 0.0 copy-start.4
  15.4 0.0 copy-start.7
  15.4 17.9 %all-to-all-done.x_ref = bf16[32,104,128]{2,1,0:T(8,128)(2,1)S(1)} async-done(((bf16[32,104,128]{2,1,0:T(8,128)(2,1)}), bf16[32,104,128]{2,1,0:T(8,128)(2,1)S(1)}, u32[]{:S(2)}, u32[]{:S(2)}) %all-to-all-start) | async-done | bytes 852000 | tf_op jit(solution)/shard_map/all_to_all | solution.py:513
  33.3 0.0 copy-done
  33.3 0.0 copy-start.5
  33.3 0.0 copy-start.6
  33.3 5.1 %transform.1 = bf16[32,72,128]{2,1,0:T(8,128)(2,1)S(1)} custom-call(bf16[32,104,128]{2,1,0:T(8,128)(2,1)S(1)} %all-to-all-done.x_ref, f32[3,8,128]{2,1,0:T(8,128)S(1)} %broadcast_multiply_fusion.own_ref, bf16[2560,256]{1,0:T(8,128)(2,1)S(1)} %copy-done), custom_call_target="tpu_custom_call" | custom-call | tf_op jit(solution)/shard_map/transform/pallas_call | solution.py:528
  38.4 20.2 %all_to_all.10.y_ref = bf16[32,72,128]{2,1,0:T(8,128)(2,1)S(1)} all-to-all(bf16[32,72,128]{2,1,0:T(8,128)(2,1)S(1)} %transform.1), channel_id=1, replica_groups=mesh['outer'=8,'inner'=4] {'outer','inner'}, dimensions={0} | all-to-all | bytes 1179648 | tf_op jit(solution)/shard_map/all_to_all | solution.py:535
  58.5 0.0 copy-done.1
  58.5 0.0 copy-done.2
  58.5 0.0 copy-done.4
  58.6 0.0 copy-done.7
  58.6 0.0 copy-done.5
  58.6 0.0 copy-done.6
  58.6 2.1 %finish.1 = (bf16[128,1024]{1,0:T(8,128)(2,1)}, bf16[128,1024]{1,0:T(8,128)(2,1)}, bf16[128,1024]{1,0:T(8,128)(2,1)}, bf16[128,1024]{1,0:T(8,128)(2,1)}) custom-call(bf16[32,72,128]{2,1,0:T(8,128)(2,1)S(1)} %all_to_all.10.y_ref, bf16[128,1024]{1,0:T(8,128)(2,1)S(1)} %copy-done.2, f32[128,1024]{1,0:T(8,128)S(1)} %copy-done.5, f32[2,128,1024]{2,1,0:T(8,128)S(1)} %copy-done.1, ...), custom_call_target="tpu_custom_call" | custom-call | tf_op jit(solution)/shard_map/finish/pallas_call | solution.py:537
  (4 shorter events, 0.0 us)
Async XLA Ops:
  3.9 7.3 %copy-start.3 = (f32[3,3,1024]{2,1,0:T(4,128)S(1)}, f32[3,3,1024]{2,1,0:T(4,128)}, u32[]{:S(2)}) copy-start(f32[3,3,1024]{2,1,0:T(4,128)} %taps_ref.3) | copy-start | bytes 110596
  4.0 29.4 %copy-start = (bf16[2560,256]{1,0:T(8,128)(2,1)S(1)}, bf16[2560,256]{1,0:T(8,128)(2,1)}, u32[]{:S(2)}) copy-start(bf16[2560,256]{1,0:T(8,128)(2,1)} %constant.22.clone.table_ref) | copy-start | bytes 3932164
  4.0 29.3 %all-to-all-start = ((bf16[32,104,128]{2,1,0:T(8,128)(2,1)}), bf16[32,104,128]{2,1,0:T(8,128)(2,1)S(1)}, u32[]{:S(2)}, u32[]{:S(2)}) async-start(bf16[32,104,128]{2,1,0:T(8,128)(2,1)} %gate.1), calls=%async_computation | async-start | bytes 1703936 | tf_op jit(solution)/shard_map/all_to_all | solution.py:513
  15.4 43.2 %copy-start.1 = (f32[2,128,1024]{2,1,0:T(8,128)S(1)}, f32[2,128,1024]{2,1,0:T(8,128)}, u32[]{:S(2)}) copy-start(f32[2,128,1024]{2,1,0:T(8,128)} %get-tuple-element.10.skv_ref) | copy-start | bytes 3145732
  15.4 43.2 %copy-start.2 = (bf16[128,1024]{1,0:T(8,128)(2,1)S(1)}, bf16[128,1024]{1,0:T(8,128)(2,1)}, u32[]{:S(2)}) copy-start(bf16[128,1024]{1,0:T(8,128)(2,1)} %g_ref.1) | copy-start | bytes 786436
  15.4 43.2 %copy-start.4 = (f32[3,3,1024]{2,1,0:T(4,128)S(1)}, f32[3,3,1024]{2,1,0:T(4,128)}, u32[]{:S(2)}) copy-start(f32[3,3,1024]{2,1,0:T(4,128)} %taps_ref.3) | copy-start | bytes 110596
  15.4 43.2 %copy-start.7 = (f32[1024]{0:T(1024)S(1)}, f32[1024]{0:T(1024)}, u32[]{:S(2)}) copy-start(f32[1024]{0:T(1024)} %param.13) | copy-start | bytes 12292
  33.3 25.3 %copy-start.5 = (f32[128,1024]{1,0:T(8,128)S(1)}, f32[128,1024]{1,0:T(8,128)}, u32[]{:S(2)}) copy-start(f32[128,1024]{1,0:T(8,128)} %get-tuple-element.9.sq_ref) | copy-start | bytes 1572868
  33.3 25.3 %copy-start.6 = (f32[3,8,1024]{2,1,0:T(8,128)S(1)}, f32[3,8,1024]{2,1,0:T(8,128)}, u32[]{:S(2)}) copy-start(f32[3,8,1024]{2,1,0:T(8,128)} %get-tuple-element.11.tail_ref) | copy-start | bytes 294916

commit v6 on v5

--- a/solution.py
+++ b/solution.py
@@ -15,7 +15,7 @@
 bf16 = jnp.bfloat16
 ITEMS = 32
 
-REACH = 240.0
+REACH = 2.0 ** (126.0 / 17.0)
 
 
 def scale_of(top):
@@ -23,16 +23,16 @@
 
 
 def encode(value, scale):
-    power = value * (REACH / scale)
-    sign = power < 0
+    base = value * (REACH / scale)
+    power = base
     for _ in range(4):
         power = power * power
-    return jnp.where(sign, -power, power)
+    return power * base
 
 
 def decode(word):
-    size = jnp.exp2(jnp.log2(jnp.abs(word)) * (1.0 / 16.0))
-    return jnp.where(word < 0, -size, size)
+    size = jnp.maximum(jnp.abs(word), 2.0**-126)
+    return word * jnp.exp2(jnp.log2(size) * (-16.0 / 17.0))
 
 
 def split_pair(value):

time: 60.9 us -> 60.8 us (level)
  no operation moved by 1% of the time
where the time goes in v6:
time: 60.8 us; the launch traced here: 60.5 us
  blocking collectives  20.2 us (33%)
  waiting for transfers between devices  17.9 us (29%)
  Pallas kernels  12.9 us (21%)
  starting transfers between devices  7.3 us (12%)
  between operations  0.76 us (1%)
  local copies, waits for them, and re-layouts  0.75 us (1%)
  other arithmetic  0.7 us (1%)
    all_to_all x1, blocking collectives, local(): returned = lax.all_to_all(result, AXES, 0, 0, tiled=True)  20.2 us
    all_to_all x1, waiting for transfers between devices, local(): spread = lax.all_to_all(packed, AXES, 0, 0, tiled=True)  17.9 us
    all_to_all x1, starting transfers between devices, local(): spread = lax.all_to_all(packed, AXES, 0, 0, tiled=True)  7.3 us
    pallas_call x1, Pallas kernels, local(): pl.pallas_call(functools.partial(transform_kernel, groups, width), out_sh...  4.97 us
    pallas_call x1, Pallas kernels, local(): pl.pallas_call(functools.partial(gate_kernel, unit), out_shape=jax.ShapeD...  3.23 us
    pallas_call x1, Pallas kernels, local(): pl.pallas_call(prepare_kernel, out_shape=(jax.ShapeDtypeStruct((rows, cha...  2.65 us
    pallas_call x1, Pallas kernels, local(): pl.pallas_call(functools.partial(finish_kernel, unit), out_shape=(wide, w...  2.09 us
  transfers between devices with their start and end apart: 1, of which 1 were waited for; matrix products, arithmetic and copies ran while one was open for 2% of the time, Pallas kernels for 4%

profile of v6, /device:TPU:0, one launch (start us, length us, event | category | flops | bytes accessed | tf_op | source)
XLA Modules:
  0.0 60.5 jit_solution(11978643529102960007)
XLA Ops:
  0.6 3.2 %gate.1 = bf16[32,104,128]{2,1,0:T(8,128)(2,1)} custom-call(bf16[128,1024]{1,0:T(8,128)(2,1)} %q_ref.1, bf16[128,1024]{1,0:T(8,128)(2,1)} %k_ref.1, bf16[128,1024]{1,0:T(8,128)(2,1)} %v_ref.1, bf16[128,1024]{1,0:T(8,128)(2,1)} %g_ref.1, f32[128,1024]{1,0:T(8,128)} %h_hbm.1, f32[3,3,1024]{2,1,0:T(4,128)} %taps_ref.3), custom_call_target="tpu_custom_call" | custom-call | tf_op jit(solution)/shard_map/gate/pallas_call | solution.py:496
  3.9 0.0 copy-start.3
  3.9 0.0 copy-start
  3.9 7.3 %all-to-all-start = ((bf16[32,104,128]{2,1,0:T(8,128)(2,1)}), bf16[32,104,128]{2,1,0:T(8,128)(2,1)S(1)}, u32[]{:S(2)}, u32[]{:S(2)}) async-start(bf16[32,104,128]{2,1,0:T(8,128)(2,1)} %gate.1), calls=%async_computation | async-start | bytes 1703936 | tf_op jit(solution)/shard_map/all_to_all | solution.py:513
  11.2 0.0 copy-done.3
  11.2 0.1 reshape.26
  11.4 0.1 dynamic-slice_reduce_fusion.2
  11.4 0.1 slice.19
  11.5 0.1 slice.21
  11.6 0.1 slice.23
  11.7 0.2 copy.16
  11.9 0.1 reshape.28
  12.0 2.7 %prepare.1 = (f32[128,1024]{1,0:T(8,128)}, f32[2,128,1024]{2,1,0:T(8,128)}, f32[3,8,1024]{2,1,0:T(8,128)}, f32[8,128]{1,0:T(8,128)}) custom-call(bf16[128,1024]{1,0:T(8,128)(2,1)} %q_ref.1, bf16[128,1024]{1,0:T(8,128)(2,1)} %k_ref.1, bf16[128,1024]{1,0:T(8,128)(2,1)} %v_ref.1, f32[3,3,1024]{2,1,0:T(4,128)} %taps_ref.3), custom_call_target="tpu_custom_call" | custom-call | flops 3932160 | bytes 2621440 | tf_op jit(solution)/shard_map/prepare/pallas_call | solution.py:514
  14.6 0.7 %broadcast_multiply_fusion.own_ref = f32[3,8,128]{2,1,0:T(8,128)S(1)} fusion(f32[3,8,128]{2,1,0:T(8,128)S(1)} %reshape.28, f32[8,128]{1,0:T(8,128)} %get-tuple-element.8), kind=kLoop, calls=%fused_computation.1 | loop fusion | flops 3072 | bytes 28672 | tf_op jit(solution)/shard_map/mul | solution.py:534
  15.3 0.0 copy-start.1
  15.3 0.0 copy-start.2
  15.3 0.0 copy-start.4
  15.3 0.0 copy-start.7
  15.3 17.9 %all-to-all-done.x_ref = bf16[32,104,128]{2,1,0:T(8,128)(2,1)S(1)} async-done(((bf16[32,104,128]{2,1,0:T(8,128)(2,1)}), bf16[32,104,128]{2,1,0:T(8,128)(2,1)S(1)}, u32[]{:S(2)}, u32[]{:S(2)}) %all-to-all-start) | async-done | bytes 852000 | tf_op jit(solution)/shard_map/all_to_all | solution.py:513
  33.2 0.0 copy-done
  33.2 0.0 copy-start.5
  33.2 0.0 copy-start.6
  33.2 5.0 %transform.1 = bf16[32,72,128]{2,1,0:T(8,128)(2,1)S(1)} custom-call(bf16[32,104,128]{2,1,0:T(8,128)(2,1)S(1)} %all-to-all-done.x_ref, f32[3,8,128]{2,1,0:T(8,128)S(1)} %broadcast_multiply_fusion.own_ref, bf16[2560,256]{1,0:T(8,128)(2,1)S(1)} %copy-done), custom_call_target="tpu_custom_call" | custom-call | tf_op jit(solution)/shard_map/transform/pallas_call | solution.py:528
  38.2 20.2 %all_to_all.10.y_ref = bf16[32,72,128]{2,1,0:T(8,128)(2,1)S(1)} all-to-all(bf16[32,72,128]{2,1,0:T(8,128)(2,1)S(1)} %transform.1), channel_id=1, replica_groups=mesh['outer'=8,'inner'=4] {'outer','inner'}, dimensions={0} | all-to-all | bytes 1179648 | tf_op jit(solution)/shard_map/all_to_all | solution.py:535
  58.4 0.0 copy-done.1
  58.4 0.0 copy-done.2
  58.4 0.0 copy-done.4
  58.4 0.0 copy-done.7
  58.4 0.0 copy-done.5
  58.4 0.0 copy-done.6
  58.4 2.1 %finish.1 = (bf16[128,1024]{1,0:T(8,128)(2,1)}, bf16[128,1024]{1,0:T(8,128)(2,1)}, bf16[128,1024]{1,0:T(8,128)(2,1)}, bf16[128,1024]{1,0:T(8,128)(2,1)}) custom-call(bf16[32,72,128]{2,1,0:T(8,128)(2,1)S(1)} %all_to_all.10.y_ref, bf16[128,1024]{1,0:T(8,128)(2,1)S(1)} %copy-done.2, f32[128,1024]{1,0:T(8,128)S(1)} %copy-done.5, f32[2,128,1024]{2,1,0:T(8,128)S(1)} %copy-done.1, ...), custom_call_target="tpu_custom_call" | custom-call | tf_op jit(solution)/shard_map/finish/pallas_call | solution.py:537
  (4 shorter events, 0.0 us)
Async XLA Ops:
  3.9 7.3 %copy-start.3 = (f32[3,3,1024]{2,1,0:T(4,128)S(1)}, f32[3,3,1024]{2,1,0:T(4,128)}, u32[]{:S(2)}) copy-start(f32[3,3,1024]{2,1,0:T(4,128)} %taps_ref.3) | copy-start | bytes 110596
  3.9 29.4 %copy-start = (bf16[2560,256]{1,0:T(8,128)(2,1)S(1)}, bf16[2560,256]{1,0:T(8,128)(2,1)}, u32[]{:S(2)}) copy-start(bf16[2560,256]{1,0:T(8,128)(2,1)} %constant.22.clone.table_ref) | copy-start | bytes 3932164
  3.9 29.3 %all-to-all-start = ((bf16[32,104,128]{2,1,0:T(8,128)(2,1)}), bf16[32,104,128]{2,1,0:T(8,128)(2,1)S(1)}, u32[]{:S(2)}, u32[]{:S(2)}) async-start(bf16[32,104,128]{2,1,0:T(8,128)(2,1)} %gate.1), calls=%async_computation | async-start | bytes 1703936 | tf_op jit(solution)/shard_map/all_to_all | solution.py:513
  15.3 43.1 %copy-start.1 = (f32[2,128,1024]{2,1,0:T(8,128)S(1)}, f32[2,128,1024]{2,1,0:T(8,128)}, u32[]{:S(2)}) copy-start(f32[2,128,1024]{2,1,0:T(8,128)} %get-tuple-element.10.skv_ref) | copy-start | bytes 3145732
  15.3 43.1 %copy-start.2 = (bf16[128,1024]{1,0:T(8,128)(2,1)S(1)}, bf16[128,1024]{1,0:T(8,128)(2,1)}, u32[]{:S(2)}) copy-start(bf16[128,1024]{1,0:T(8,128)(2,1)} %g_ref.1) | copy-start | bytes 786436
  15.3 43.1 %copy-start.4 = (f32[3,3,1024]{2,1,0:T(4,128)S(1)}, f32[3,3,1024]{2,1,0:T(4,128)}, u32[]{:S(2)}) copy-start(f32[3,3,1024]{2,1,0:T(4,128)} %taps_ref.3) | copy-start | bytes 110596
  15.3 43.1 %copy-start.7 = (f32[1024]{0:T(1024)S(1)}, f32[1024]{0:T(1024)}, u32[]{:S(2)}) copy-start(f32[1024]{0:T(1024)} %param.13) | copy-start | bytes 12292
  33.2 25.2 %copy-start.5 = (f32[128,1024]{1,0:T(8,128)S(1)}, f32[128,1024]{1,0:T(8,128)}, u32[]{:S(2)}) copy-start(f32[128,1024]{1,0:T(8,128)} %get-tuple-element.9.sq_ref) | copy-start | bytes 1572868
  33.2 25.2 %copy-start.6 = (f32[3,8,1024]{2,1,0:T(8,128)S(1)}, f32[3,8,1024]{2,1,0:T(8,128)}, u32[]{:S(2)}) copy-start(f32[3,8,1024]{2,1,0:T(8,128)} %get-tuple-element.11.tail_ref) | copy-start | bytes 294916

commit v7 on v6

--- a/solution.py
+++ b/solution.py
@@ -19,7 +19,10 @@
 
 
 def scale_of(top):
-    return jnp.maximum(top, 2.0**-100).astype(bf16).astype(f32)
+    top = jnp.maximum(top, 2.0**-100)
+    high = top.astype(bf16).astype(f32)
+    low = (top - high).astype(bf16).astype(f32)
+    return high + low, high, low
 
 
 def encode(value, scale):
@@ -220,8 +223,9 @@
         if which != 1:
             edge = jnp.where(row < 2, 0.0, signal[:8])
             signal = jnp.concatenate([edge, signal[8:]], axis=0)
-        scale = scale_of(jnp.max(jnp.abs(signal), axis=0, keepdims=True))
-        extra[14 + which : 15 + which, lanes] = scale
+        scale, high, low = scale_of(jnp.max(jnp.abs(signal), axis=0, keepdims=True))
+        extra[14 + which : 15 + which, lanes] = high
+        extra[17 + which : 18 + which, lanes] = low
         words = encode(signal, scale)
         if run % 16 == 0:
             words = words.astype(bf16).T.reshape(chunk // run, run, rows)
@@ -307,7 +311,8 @@
         for at in range(together):
             part = both[:, at * unit : (at + 1) * unit, :].reshape(count, rows)
             left = ITEMS * (base + at)
-            scale = extra[:, left + 14 + which : left + 15 + which] * (1.0 / REACH)
+            scale = extra[:, left + 14 + which : left + 15 + which]
+            scale = (scale + extra[:, left + 17 + which : left + 18 + which]) * (1.0 / REACH)
             signal = decode(part) * scale
             if which == 0:
                 signal = jnp.where(lane < 2, turn(edge_gated, -left), signal)
@@ -350,7 +355,7 @@
             for at in range(together):
                 here = slice((2 * at + which) * rows, (2 * at + which + 1) * rows)
                 part = result[:, here].reshape(blocks, unit, rows)
-                scale = scale_of(
+                scale, *halves = scale_of(
                     jnp.max(jnp.max(jnp.abs(part), axis=0), axis=1, keepdims=True)
                 )
                 words = encode(part, scale[None])
@@ -358,9 +363,10 @@
                 left = ITEMS * (base + at) + 16 + 2 * which
                 mine = turn(words.reshape(count, rows), left)
                 placed = jnp.where((lane >= left) & (lane < left + 2), mine, placed)
-                spot = ITEMS * (base + at) + 20 + which
-                all_scale = jnp.broadcast_to(scale[None], (blocks, unit, rows))
-                placed = jnp.where(lane == spot, all_scale.reshape(count, rows), placed)
+                spot = lane - (ITEMS * (base + at) + 20 + which)
+                for nth, half in enumerate(halves):
+                    value = jnp.broadcast_to(half[None], (blocks, unit, rows))
+                    placed = jnp.where(spot == 2 * nth, value.reshape(count, rows), placed)
             out_ref[:, pl.ds(which * width + base * unit, together * unit), :] = jnp.concatenate(
                 pieces, axis=1
             ).astype(bf16)
@@ -417,7 +423,8 @@
                 part = part.reshape(chunk, rows).T.astype(f32)
             else:
                 part = part.astype(f32).reshape(chunk, rows).T
-            scale = items[20 + which : 21 + which] * (1.0 / REACH)
+            scale = items[20 + which : 21 + which] + items[22 + which : 23 + which]
+            scale = scale * (1.0 / REACH)
             return decode(part) * scale, decode(items[16 + 2 * which : 18 + 2 * which]) * scale
 
         upstream = g_ref[:, lanes].astype(f32)

time: 60.8 us -> 60.8 us (level)
  no operation moved by 1% of the time
where the time goes in v7:
time: 60.8 us; the launch traced here: 60.5 us
  blocking collectives  20.2 us (33%)
  waiting for transfers between devices  17.9 us (29%)
  Pallas kernels  13 us (21%)
  starting transfers between devices  7.3 us (12%)
  between operations  0.76 us (1%)
  local copies, waits for them, and re-layouts  0.75 us (1%)
  other arithmetic  0.7 us (1%)
    all_to_all x1, blocking collectives, local(): returned = lax.all_to_all(result, AXES, 0, 0, tiled=True)  20.2 us
    all_to_all x1, waiting for transfers between devices, local(): spread = lax.all_to_all(packed, AXES, 0, 0, tiled=True)  17.9 us
    all_to_all x1, starting transfers between devices, local(): spread = lax.all_to_all(packed, AXES, 0, 0, tiled=True)  7.3 us
    pallas_call x1, Pallas kernels, local(): pl.pallas_call(functools.partial(transform_kernel, groups, width), out_sh...  5.01 us
    pallas_call x1, Pallas kernels, local(): pl.pallas_call(functools.partial(gate_kernel, unit), out_shape=jax.ShapeD...  3.24 us
    pallas_call x1, Pallas kernels, local(): pl.pallas_call(prepare_kernel, out_shape=(jax.ShapeDtypeStruct((rows, cha...  2.65 us
    pallas_call x1, Pallas kernels, local(): pl.pallas_call(functools.partial(finish_kernel, unit), out_shape=(wide, w...  2.09 us
  transfers between devices with their start and end apart: 1, of which 1 were waited for; matrix products, arithmetic and copies ran while one was open for 2% of the time, Pallas kernels for 4%

profile of v7, /device:TPU:0, one launch (start us, length us, event | category | flops | bytes accessed | tf_op | source)
XLA Modules:
  0.0 60.5 jit_solution(15175938519240474862)
XLA Ops:
  0.6 3.2 %gate.1 = bf16[32,104,128]{2,1,0:T(8,128)(2,1)} custom-call(bf16[128,1024]{1,0:T(8,128)(2,1)} %q_ref.1, bf16[128,1024]{1,0:T(8,128)(2,1)} %k_ref.1, bf16[128,1024]{1,0:T(8,128)(2,1)} %v_ref.1, bf16[128,1024]{1,0:T(8,128)(2,1)} %g_ref.1, f32[128,1024]{1,0:T(8,128)} %h_hbm.1, f32[3,3,1024]{2,1,0:T(4,128)} %taps_ref.3), custom_call_target="tpu_custom_call" | custom-call | tf_op jit(solution)/shard_map/gate/pallas_call | solution.py:503
  3.9 0.0 copy-start.3
  3.9 0.0 copy-start
  3.9 7.3 %all-to-all-start = ((bf16[32,104,128]{2,1,0:T(8,128)(2,1)}), bf16[32,104,128]{2,1,0:T(8,128)(2,1)S(1)}, u32[]{:S(2)}, u32[]{:S(2)}) async-start(bf16[32,104,128]{2,1,0:T(8,128)(2,1)} %gate.1), calls=%async_computation | async-start | bytes 1703936 | tf_op jit(solution)/shard_map/all_to_all | solution.py:520
  11.2 0.0 copy-done.3
  11.2 0.1 reshape.26
  11.4 0.1 dynamic-slice_reduce_fusion.2
  11.4 0.1 slice.19
  11.5 0.1 slice.21
  11.6 0.1 slice.23
  11.7 0.2 copy.16
  11.9 0.1 reshape.28
  12.0 2.7 %prepare.1 = (f32[128,1024]{1,0:T(8,128)}, f32[2,128,1024]{2,1,0:T(8,128)}, f32[3,8,1024]{2,1,0:T(8,128)}, f32[8,128]{1,0:T(8,128)}) custom-call(bf16[128,1024]{1,0:T(8,128)(2,1)} %q_ref.1, bf16[128,1024]{1,0:T(8,128)(2,1)} %k_ref.1, bf16[128,1024]{1,0:T(8,128)(2,1)} %v_ref.1, f32[3,3,1024]{2,1,0:T(4,128)} %taps_ref.3), custom_call_target="tpu_custom_call" | custom-call | flops 3932160 | bytes 2621440 | tf_op jit(solution)/shard_map/prepare/pallas_call | solution.py:521
  14.6 0.7 %broadcast_multiply_fusion.own_ref = f32[3,8,128]{2,1,0:T(8,128)S(1)} fusion(f32[3,8,128]{2,1,0:T(8,128)S(1)} %reshape.28, f32[8,128]{1,0:T(8,128)} %get-tuple-element.8), kind=kLoop, calls=%fused_computation.1 | loop fusion | flops 3072 | bytes 28672 | tf_op jit(solution)/shard_map/mul | solution.py:541
  15.3 0.0 copy-start.1
  15.3 0.0 copy-start.2
  15.3 0.0 copy-start.4
  15.3 0.0 copy-start.7
  15.3 17.9 %all-to-all-done.x_ref = bf16[32,104,128]{2,1,0:T(8,128)(2,1)S(1)} async-done(((bf16[32,104,128]{2,1,0:T(8,128)(2,1)}), bf16[32,104,128]{2,1,0:T(8,128)(2,1)S(1)}, u32[]{:S(2)}, u32[]{:S(2)}) %all-to-all-start) | async-done | bytes 852000 | tf_op jit(solution)/shard_map/all_to_all | solution.py:520
  33.2 0.0 copy-done
  33.2 0.0 copy-start.5
  33.2 0.0 copy-start.6
  33.2 5.0 %transform.1 = bf16[32,72,128]{2,1,0:T(8,128)(2,1)S(1)} custom-call(bf16[32,104,128]{2,1,0:T(8,128)(2,1)S(1)} %all-to-all-done.x_ref, f32[3,8,128]{2,1,0:T(8,128)S(1)} %broadcast_multiply_fusion.own_ref, bf16[2560,256]{1,0:T(8,128)(2,1)S(1)} %copy-done), custom_call_target="tpu_custom_call" | custom-call | tf_op jit(solution)/shard_map/transform/pallas_call | solution.py:535
  38.3 20.2 %all_to_all.10.y_ref = bf16[32,72,128]{2,1,0:T(8,128)(2,1)S(1)} all-to-all(bf16[32,72,128]{2,1,0:T(8,128)(2,1)S(1)} %transform.1), channel_id=1, replica_groups=mesh['outer'=8,'inner'=4] {'outer','inner'}, dimensions={0} | all-to-all | bytes 1179648 | tf_op jit(solution)/shard_map/all_to_all | solution.py:542
  58.4 0.0 copy-done.1
  58.4 0.0 copy-done.2
  58.4 0.0 copy-done.4
  58.4 0.0 copy-done.7
  58.4 0.0 copy-done.5
  58.4 0.0 copy-done.6
  58.5 2.1 %finish.1 = (bf16[128,1024]{1,0:T(8,128)(2,1)}, bf16[128,1024]{1,0:T(8,128)(2,1)}, bf16[128,1024]{1,0:T(8,128)(2,1)}, bf16[128,1024]{1,0:T(8,128)(2,1)}) custom-call(bf16[32,72,128]{2,1,0:T(8,128)(2,1)S(1)} %all_to_all.10.y_ref, bf16[128,1024]{1,0:T(8,128)(2,1)S(1)} %copy-done.2, f32[128,1024]{1,0:T(8,128)S(1)} %copy-done.5, f32[2,128,1024]{2,1,0:T(8,128)S(1)} %copy-done.1, ...), custom_call_target="tpu_custom_call" | custom-call | tf_op jit(solution)/shard_map/finish/pallas_call | solution.py:544
  (4 shorter events, 0.0 us)
Async XLA Ops:
  3.9 7.3 %copy-start.3 = (f32[3,3,1024]{2,1,0:T(4,128)S(1)}, f32[3,3,1024]{2,1,0:T(4,128)}, u32[]{:S(2)}) copy-start(f32[3,3,1024]{2,1,0:T(4,128)} %taps_ref.3) | copy-start | bytes 110596
  3.9 29.4 %copy-start = (bf16[2560,256]{1,0:T(8,128)(2,1)S(1)}, bf16[2560,256]{1,0:T(8,128)(2,1)}, u32[]{:S(2)}) copy-start(bf16[2560,256]{1,0:T(8,128)(2,1)} %constant.22.clone.table_ref) | copy-start | bytes 3932164
  3.9 29.3 %all-to-all-start = ((bf16[32,104,128]{2,1,0:T(8,128)(2,1)}), bf16[32,104,128]{2,1,0:T(8,128)(2,1)S(1)}, u32[]{:S(2)}, u32[]{:S(2)}) async-start(bf16[32,104,128]{2,1,0:T(8,128)(2,1)} %gate.1), calls=%async_computation | async-start | bytes 1703936 | tf_op jit(solution)/shard_map/all_to_all | solution.py:520
  15.3 43.1 %copy-start.1 = (f32[2,128,1024]{2,1,0:T(8,128)S(1)}, f32[2,128,1024]{2,1,0:T(8,128)}, u32[]{:S(2)}) copy-start(f32[2,128,1024]{2,1,0:T(8,128)} %get-tuple-element.10.skv_ref) | copy-start | bytes 3145732
  15.3 43.1 %copy-start.2 = (bf16[128,1024]{1,0:T(8,128)(2,1)S(1)}, bf16[128,1024]{1,0:T(8,128)(2,1)}, u32[]{:S(2)}) copy-start(bf16[128,1024]{1,0:T(8,128)(2,1)} %g_ref.1) | copy-start | bytes 786436
  15.3 43.1 %copy-start.4 = (f32[3,3,1024]{2,1,0:T(4,128)S(1)}, f32[3,3,1024]{2,1,0:T(4,128)}, u32[]{:S(2)}) copy-start(f32[3,3,1024]{2,1,0:T(4,128)} %taps_ref.3) | copy-start | bytes 110596
  15.3 43.1 %copy-start.7 = (f32[1024]{0:T(1024)S(1)}, f32[1024]{0:T(1024)}, u32[]{:S(2)}) copy-start(f32[1024]{0:T(1024)} %param.13) | copy-start | bytes 12292
  33.2 25.2 %copy-start.5 = (f32[128,1024]{1,0:T(8,128)S(1)}, f32[128,1024]{1,0:T(8,128)}, u32[]{:S(2)}) copy-start(f32[128,1024]{1,0:T(8,128)} %get-tuple-element.9.sq_ref) | copy-start | bytes 1572868
  33.2 25.2 %copy-start.6 = (f32[3,8,1024]{2,1,0:T(8,128)S(1)}, f32[3,8,1024]{2,1,0:T(8,128)}, u32[]{:S(2)}) copy-start(f32[3,8,1024]{2,1,0:T(8,128)} %get-tuple-element.11.tail_ref) | copy-start | bytes 294916

commit v8 on v7

--- a/solution.py
+++ b/solution.py
@@ -170,16 +170,6 @@
 
 def taps_at(taps_ref, which, lanes):
     return [taps_ref[which, tap : tap + 1, lanes] for tap in range(3)]
-
-
-def ahead(rows, steps, rim):
-    count = rows.shape[0]
-    rolled = pltpu.roll(rows, count - steps, 0)
-    edge = rolled[count - 8 :]
-    row = lax.broadcasted_iota(jnp.int32, edge.shape, 0)
-    for at in range(steps):
-        edge = jnp.where(row == 8 - steps + at, rim[at : at + 1], edge)
-    return jnp.concatenate([rolled[: count - 8], edge], axis=0)
 
 
 def slices_of(channels):
@@ -393,7 +383,7 @@
 def finish_kernel(
     unit, y_ref, g_ref, sq_ref, skv_ref, tail_ref, taps_ref, skip_ref, *refs
 ):
-    targets, held, sems = refs[:4], refs[4:8], refs[8]
+    targets, held, sems, window = refs[:4], refs[4:8], refs[8], refs[9]
     rows, channels = g_ref.shape
     blocks = y_ref.shape[0]
     width = channels // blocks
@@ -461,8 +451,11 @@
         for which in range(3):
             rows_of, rim = grads[which]
             one, two, three = taps[which]
+            view = window.at[start // chunk % 2 * 3 + which]
+            view[:rows] = rows_of
+            view[rows : rows + 2] = rim
             held[1 + which][:, lanes] = (
-                one * rows_of + two * ahead(rows_of, 1, rim) + three * ahead(rows_of, 2, rim)
+                one * rows_of + two * view[1 : rows + 1] + three * view[2 : rows + 2]
             ).astype(bf16)
         if (start + chunk) % slices[0].size == 0:
             at = start // slices[0].size
@@ -546,7 +539,11 @@
         out_shape=(wide, wide, wide, wide),
         in_specs=[near] * 7,
         out_specs=(far, far, far, far),
-        scratch_shapes=[*[stream] * 4, pltpu.SemaphoreType.DMA((parts, 4))],
+        scratch_shapes=[
+            *[stream] * 4,
+            pltpu.SemaphoreType.DMA((parts, 4)),
+            pltpu.VMEM((6, rows + 8, 128), f32),
+        ],
         compiler_params=small,
         name="finish",
     )(returned, grad_out, *short, tail, conv_taps, skip)

time: 60.8 us -> 60.8 us (level)
  no operation moved by 1% of the time
where the time goes in v8:
time: 60.8 us; the launch traced here: 60.5 us
  blocking collectives  20.2 us (33%)
  waiting for transfers between devices  17.9 us (29%)
  Pallas kernels  12.9 us (21%)
  starting transfers between devices  7.3 us (12%)
  between operations  0.76 us (1%)
  local copies, waits for them, and re-layouts  0.75 us (1%)
  other arithmetic  0.7 us (1%)
    all_to_all x1, blocking collectives, local(): returned = lax.all_to_all(result, AXES, 0, 0, tiled=True)  20.2 us
    all_to_all x1, waiting for transfers between devices, local(): spread = lax.all_to_all(packed, AXES, 0, 0, tiled=True)  17.9 us
    all_to_all x1, starting transfers between devices, local(): spread = lax.all_to_all(packed, AXES, 0, 0, tiled=True)  7.3 us
    pallas_call x1, Pallas kernels, local(): pl.pallas_call(functools.partial(transform_kernel, groups, width), out_sh...  5.01 us
    pallas_call x1, Pallas kernels, local(): pl.pallas_call(functools.partial(gate_kernel, unit), out_shape=jax.ShapeD...  3.24 us
    pallas_call x1, Pallas kernels, local(): pl.pallas_call(prepare_kernel, out_shape=(jax.ShapeDtypeStruct((rows, cha...  2.65 us
    pallas_call x1, Pallas kernels, local(): pl.pallas_call(functools.partial(finish_kernel, unit), out_shape=(wide, w...  2.05 us
  transfers between devices with their start and end apart: 1, of which 1 were waited for; matrix products, arithmetic and copies ran while one was open for 2% of the time, Pallas kernels for 4%

profile of v8, /device:TPU:0, one launch (start us, length us, event | category | flops | bytes accessed | tf_op | source)
XLA Modules:
  0.0 60.5 jit_solution(6849867585221602562)
XLA Ops:
  0.6 3.2 %gate.1 = bf16[32,104,128]{2,1,0:T(8,128)(2,1)} custom-call(bf16[128,1024]{1,0:T(8,128)(2,1)} %q_ref.1, bf16[128,1024]{1,0:T(8,128)(2,1)} %k_ref.1, bf16[128,1024]{1,0:T(8,128)(2,1)} %v_ref.1, bf16[128,1024]{1,0:T(8,128)(2,1)} %g_ref.1, f32[128,1024]{1,0:T(8,128)} %h_hbm.1, f32[3,3,1024]{2,1,0:T(4,128)} %taps_ref.3), custom_call_target="tpu_custom_call" | custom-call | tf_op jit(solution)/shard_map/gate/pallas_call | solution.py:496
  3.9 0.0 copy-start.3
  3.9 0.0 copy-start
  3.9 7.3 %all-to-all-start = ((bf16[32,104,128]{2,1,0:T(8,128)(2,1)}), bf16[32,104,128]{2,1,0:T(8,128)(2,1)S(1)}, u32[]{:S(2)}, u32[]{:S(2)}) async-start(bf16[32,104,128]{2,1,0:T(8,128)(2,1)} %gate.1), calls=%async_computation | async-start | bytes 1703936 | tf_op jit(solution)/shard_map/all_to_all | solution.py:513
  11.2 0.0 copy-done.3
  11.2 0.1 reshape.26
  11.4 0.1 dynamic-slice_reduce_fusion.2
  11.4 0.1 slice.19
  11.5 0.1 slice.21
  11.6 0.1 slice.23
  11.7 0.2 copy.16
  11.9 0.1 reshape.28
  12.0 2.7 %prepare.1 = (f32[128,1024]{1,0:T(8,128)}, f32[2,128,1024]{2,1,0:T(8,128)}, f32[3,8,1024]{2,1,0:T(8,128)}, f32[8,128]{1,0:T(8,128)}) custom-call(bf16[128,1024]{1,0:T(8,128)(2,1)} %q_ref.1, bf16[128,1024]{1,0:T(8,128)(2,1)} %k_ref.1, bf16[128,1024]{1,0:T(8,128)(2,1)} %v_ref.1, f32[3,3,1024]{2,1,0:T(4,128)} %taps_ref.3), custom_call_target="tpu_custom_call" | custom-call | flops 3932160 | bytes 2621440 | tf_op jit(solution)/shard_map/prepare/pallas_call | solution.py:514
  14.6 0.7 %broadcast_multiply_fusion.own_ref = f32[3,8,128]{2,1,0:T(8,128)S(1)} fusion(f32[3,8,128]{2,1,0:T(8,128)S(1)} %reshape.28, f32[8,128]{1,0:T(8,128)} %get-tuple-element.8), kind=kLoop, calls=%fused_computation.1 | loop fusion | flops 3072 | bytes 28672 | tf_op jit(solution)/shard_map/mul | solution.py:534
  15.3 0.0 copy-start.1
  15.3 0.0 copy-start.2
  15.3 0.0 copy-start.4
  15.3 0.0 copy-start.7
  15.3 17.9 %all-to-all-done.x_ref = bf16[32,104,128]{2,1,0:T(8,128)(2,1)S(1)} async-done(((bf16[32,104,128]{2,1,0:T(8,128)(2,1)}), bf16[32,104,128]{2,1,0:T(8,128)(2,1)S(1)}, u32[]{:S(2)}, u32[]{:S(2)}) %all-to-all-start) | async-done | bytes 852000 | tf_op jit(solution)/shard_map/all_to_all | solution.py:513
  33.2 0.0 copy-done
  33.2 0.0 copy-start.5
  33.2 0.0 copy-start.6
  33.2 5.0 %transform.1 = bf16[32,72,128]{2,1,0:T(8,128)(2,1)S(1)} custom-call(bf16[32,104,128]{2,1,0:T(8,128)(2,1)S(1)} %all-to-all-done.x_ref, f32[3,8,128]{2,1,0:T(8,128)S(1)} %broadcast_multiply_fusion.own_ref, bf16[2560,256]{1,0:T(8,128)(2,1)S(1)} %copy-done), custom_call_target="tpu_custom_call" | custom-call | tf_op jit(solution)/shard_map/transform/pallas_call | solution.py:528
  38.3 20.2 %all_to_all.10.y_ref = bf16[32,72,128]{2,1,0:T(8,128)(2,1)S(1)} all-to-all(bf16[32,72,128]{2,1,0:T(8,128)(2,1)S(1)} %transform.1), channel_id=1, replica_groups=mesh['outer'=8,'inner'=4] {'outer','inner'}, dimensions={0} | all-to-all | bytes 1179648 | tf_op jit(solution)/shard_map/all_to_all | solution.py:535
  58.4 0.0 copy-done.1
  58.4 0.0 copy-done.2
  58.4 0.0 copy-done.4
  58.4 0.0 copy-done.7
  58.4 0.0 copy-done.5
  58.4 0.0 copy-done.6
  58.5 2.0 %finish.1 = (bf16[128,1024]{1,0:T(8,128)(2,1)}, bf16[128,1024]{1,0:T(8,128)(2,1)}, bf16[128,1024]{1,0:T(8,128)(2,1)}, bf16[128,1024]{1,0:T(8,128)(2,1)}) custom-call(bf16[32,72,128]{2,1,0:T(8,128)(2,1)S(1)} %all_to_all.10.y_ref, bf16[128,1024]{1,0:T(8,128)(2,1)S(1)} %copy-done.2, f32[128,1024]{1,0:T(8,128)S(1)} %copy-done.5, f32[2,128,1024]{2,1,0:T(8,128)S(1)} %copy-done.1, ...), custom_call_target="tpu_custom_call" | custom-call | tf_op jit(solution)/shard_map/finish/pallas_call | solution.py:537
  (4 shorter events, 0.0 us)
Async XLA Ops:
  3.9 7.3 %copy-start.3 = (f32[3,3,1024]{2,1,0:T(4,128)S(1)}, f32[3,3,1024]{2,1,0:T(4,128)}, u32[]{:S(2)}) copy-start(f32[3,3,1024]{2,1,0:T(4,128)} %taps_ref.3) | copy-start | bytes 110596
  3.9 29.4 %copy-start = (bf16[2560,256]{1,0:T(8,128)(2,1)S(1)}, bf16[2560,256]{1,0:T(8,128)(2,1)}, u32[]{:S(2)}) copy-start(bf16[2560,256]{1,0:T(8,128)(2,1)} %constant.22.clone.table_ref) | copy-start | bytes 3932164
  3.9 29.3 %all-to-all-start = ((bf16[32,104,128]{2,1,0:T(8,128)(2,1)}), bf16[32,104,128]{2,1,0:T(8,128)(2,1)S(1)}, u32[]{:S(2)}, u32[]{:S(2)}) async-start(bf16[32,104,128]{2,1,0:T(8,128)(2,1)} %gate.1), calls=%async_computation | async-start | bytes 1703936 | tf_op jit(solution)/shard_map/all_to_all | solution.py:513
  15.3 43.1 %copy-start.1 = (f32[2,128,1024]{2,1,0:T(8,128)S(1)}, f32[2,128,1024]{2,1,0:T(8,128)}, u32[]{:S(2)}) copy-start(f32[2,128,1024]{2,1,0:T(8,128)} %get-tuple-element.10.skv_ref) | copy-start | bytes 3145732
  15.3 43.1 %copy-start.2 = (bf16[128,1024]{1,0:T(8,128)(2,1)S(1)}, bf16[128,1024]{1,0:T(8,128)(2,1)}, u32[]{:S(2)}) copy-start(bf16[128,1024]{1,0:T(8,128)(2,1)} %g_ref.1) | copy-start | bytes 786436
  15.3 43.1 %copy-start.4 = (f32[3,3,1024]{2,1,0:T(4,128)S(1)}, f32[3,3,1024]{2,1,0:T(4,128)}, u32[]{:S(2)}) copy-start(f32[3,3,1024]{2,1,0:T(4,128)} %taps_ref.3) | copy-start | bytes 110596
  15.3 43.1 %copy-start.7 = (f32[1024]{0:T(1024)S(1)}, f32[1024]{0:T(1024)}, u32[]{:S(2)}) copy-start(f32[1024]{0:T(1024)} %param.13) | copy-start | bytes 12292
  33.2 25.2 %copy-start.5 = (f32[128,1024]{1,0:T(8,128)S(1)}, f32[128,1024]{1,0:T(8,128)}, u32[]{:S(2)}) copy-start(f32[128,1024]{1,0:T(8,128)} %get-tuple-element.9.sq_ref) | copy-start | bytes 1572868
  33.2 25.2 %copy-start.6 = (f32[3,8,1024]{2,1,0:T(8,128)S(1)}, f32[3,8,1024]{2,1,0:T(8,128)}, u32[]{:S(2)}) copy-start(f32[3,8,1024]{2,1,0:T(8,128)} %get-tuple-element.11.tail_ref) | copy-start | bytes 294916
